TPU v7x, 256 devices: a whole 4x4x8 slice. The times are simulated.
256 devices in a mesh: dp: 16 (over z, core), tensor: 16 (over x, y).
Axes of the slice: x: 4, y: 4, z: 8, core: 2. Of those that a mesh axis runs over, the one named last changes fastest.
Arguments:
- grad_kv: bfloat16 [16, 8192, 2048], P('dp', None, 'tensor'), may hold values from -6 to 6
- error_kv: bfloat16 [16, 8192, 2048], P('dp', None, 'tensor'), may hold values from -6 to 6
- grad_out: bfloat16 [16, 4096, 4096], P('dp', 'tensor'), may hold values from -6 to 6
- error_out: bfloat16 [16, 4096, 4096], P('dp', 'tensor'), may hold values from -6 to 6
- warm_kv: float32 [2048, 8], P('tensor'), may hold values from -6 to 6
- warm_out: float32 [4096, 8], replicated, may hold values from -6 to 6
Outputs:
- factor_kv: float32 [2048, 8], P('tensor')
- factor_out: float32 [4096, 8], replicated
- residual_kv: bfloat16 [16, 8192, 2048], P('dp', None, 'tensor')
- residual_out: bfloat16 [16, 4096, 4096], P('dp', 'tensor')
All inputs are finite; a program needn't handle non-finite values.
Results may differ from a plain program's by a relative error of at most 0.012.
Values sent between devices are 32-bit elements; how exact they have to be, the bound alone decides.
No kernel may reach another device: no remote copies, remote signals or barrier semaphores. Data moves between devices by JAX's collectives and lax.ppermute only.
A program may use at most 64 MiB of HBM per device.

v0:
```python
import jax
import jax.numpy as jnp
from jax import lax
from jax.sharding import PartitionSpec as P

epsilon = 1e-06
highest = lax.Precision.HIGHEST


def projection_total(values):
    return lax.psum(values, "tensor")


def length_total(values):
    return lax.psum(values, "tensor")


def combine(values, sharded, summer):
    picked = tuple((value for value, flag in zip(values, sharded) if flag))
    totals = summer(picked)
    result = []
    position = 0
    for value, flag in zip(values, sharded):
        if flag:
            result.append(totals[position])
            position = position + 1
        else:
            result.append(value)
    return tuple(result)


def orthonormal(sketches, sharded):
    columns = sketches[0].shape[1]
    built = [[] for sketch in sketches]
    for column in range(columns):
        vectors = [sketch[:, column] for sketch in sketches]
        if column > 0:
            earlier = [jnp.stack(done, axis=1) for done in built]
            inner = tuple(
                (
                    jnp.dot(prior.T, vector, precision=highest, preferred_element_type=jnp.float32)
                    for prior, vector in zip(earlier, vectors)
                )
            )
            inner = combine(inner, sharded, projection_total)
            vectors = [
                vector
                - jnp.dot(prior, weights, precision=highest, preferred_element_type=jnp.float32)
                for vector, prior, weights in zip(vectors, earlier, inner)
            ]
        squares = tuple((jnp.sum(vector * vector) for vector in vectors))
        squares = combine(squares, sharded, length_total)
        for done, vector, square in zip(built, vectors, squares):
            done.append(vector * lax.rsqrt(square + epsilon))
    return tuple((jnp.stack(done, axis=1) for done in built))


def per_device(grad_kv, error_kv, grad_out, error_out, warm_kv, warm_out):
    merged_kv = (grad_kv[0].astype(jnp.float32) + error_kv[0].astype(jnp.float32)).astype(
        jnp.bfloat16
    )
    merged_out = (grad_out[0].astype(jnp.float32) + error_out[0].astype(jnp.float32)).astype(
        jnp.bfloat16
    )
    partial_kv = jnp.dot(
        merged_kv, warm_kv.astype(jnp.bfloat16), preferred_element_type=jnp.float32
    )
    partial_out = jnp.dot(
        merged_out, warm_out.astype(jnp.bfloat16), preferred_element_type=jnp.float32
    )
    sketch_kv = lax.psum(partial_kv, ("dp", "tensor"))
    sketch_out = lax.psum(partial_out, "dp")
    basis_kv, basis_out = orthonormal((sketch_kv, sketch_out), (False, True))
    replicas = lax.axis_size("dp")
    term_kv = lax.dot_general(
        merged_kv,
        basis_kv.astype(jnp.bfloat16),
        (((0,), (0,)), ((), ())),
        preferred_element_type=jnp.float32,
    )
    term_out = lax.dot_general(
        merged_out,
        basis_out.astype(jnp.bfloat16),
        (((0,), (0,)), ((), ())),
        preferred_element_type=jnp.float32,
    )
    factor_kv = lax.psum(term_kv, "dp") / replicas
    factor_out = lax.psum(term_out, ("dp", "tensor")) / replicas
    approx_kv = jnp.dot(
        basis_kv, factor_kv.T, precision=highest, preferred_element_type=jnp.float32
    )
    approx_out = jnp.dot(
        basis_out, factor_out.T, precision=highest, preferred_element_type=jnp.float32
    )
    residual_kv = (merged_kv.astype(jnp.float32) - approx_kv).astype(jnp.bfloat16)[None]
    residual_out = (merged_out.astype(jnp.float32) - approx_out).astype(jnp.bfloat16)[None]
    return (factor_kv, factor_out, residual_kv, residual_out)


def solution(mesh):
    placed = (
        P("dp", None, "tensor"),
        P("dp", None, "tensor"),
        P("dp", "tensor", None),
        P("dp", "tensor", None),
        P("tensor", None),
        P(),
    )
    return jax.shard_map(
        per_device,
        mesh=mesh,
        in_specs=placed,
        out_specs=(P("tensor", None), P(), P("dp", None, "tensor"), P("dp", "tensor", None)),
        check_vma=False,
    )
```

profile of v0, /device:TPU:1, one launch (start us, length us, event | category | flops | bytes accessed | tf_op | source)
XLA Modules:
  0.0 929.4 jit_solution(8784947719975286017)
XLA Ops:
  7.2 2.9 fusion.14
  10.1 27.9 %psum.135 = f32[256,8]{0,1:T(8,128)S(1)} all-reduce(f32[256,8]{0,1:T(8,128)S(1)} %fusion.14), channel_id=1, replica_groups=mesh['dp'=16,'tensor'=16] {'dp'}, use_global_device_ids=true, to_apply=%region_10.0 | all-reduce | flops 2048 | bytes 16384 | tf_op jit(solution)/shard_map/psum | solution.py:72
  38.6 34.5 %psum.136 = f32[]{:T(128)} all-reduce(f32[]{:T(128)} %multiply_reduce_fusion.17), channel_id=1, replica_groups=mesh['dp'=16,'tensor'=16] {'tensor'}, use_global_device_ids=true, to_apply=%region_12.0 | all-reduce | flops 1 | bytes 8 | tf_op jit(solution)/shard_map/psum | solution.py:15
  74.4 29.2 %psum.137 = f32[]{:T(128)} all-reduce(f32[]{:T(128)} %multiply_reduce_fusion.9), channel_id=1, replica_groups=mesh['dp'=16,'tensor'=16] {'tensor'}, use_global_device_ids=true, to_apply=%region_13.0 | all-reduce | flops 1 | bytes 8 | tf_op jit(solution)/shard_map/psum | solution.py:11
  103.6 1.2 multiply_reduce_fusion.16
  104.8 30.8 %psum.138 = f32[]{:T(128)} all-reduce(f32[]{:T(128)} %multiply_reduce_fusion.16), channel_id=1, replica_groups=mesh['dp'=16,'tensor'=16] {'tensor'}, use_global_device_ids=true, to_apply=%region_15.0 | all-reduce | flops 1 | bytes 8 | tf_op jit(solution)/shard_map/psum | solution.py:15
  136.3 0.7 broadcast_multiply_fusion.15
  137.1 28.5 %psum.139 = f32[2]{0:T(128)S(1)} all-reduce(f32[2]{0:T(128)S(1)} %convolution_bitcast_fusion.5), channel_id=1, replica_groups=mesh['dp'=16,'tensor'=16] {'tensor'}, use_global_device_ids=true, to_apply=%region_16.0 | all-reduce | flops 2 | bytes 16 | tf_op jit(solution)/shard_map/psum | solution.py:11
  165.8 0.6 multiply_reduce_fusion.15
  166.4 31.0 %psum.140 = f32[]{:T(128)} all-reduce(f32[]{:T(128)} %get-tuple-element.28), channel_id=1, replica_groups=mesh['dp'=16,'tensor'=16] {'tensor'}, use_global_device_ids=true, to_apply=%region_18.0 | all-reduce | flops 1 | bytes 8 | tf_op jit(solution)/shard_map/psum | solution.py:15
  198.3 28.5 %psum.141 = f32[3]{0:T(128)S(1)} all-reduce(f32[3]{0:T(128)S(1)} %convolution_bitcast_fusion.4), channel_id=1, replica_groups=mesh['dp'=16,'tensor'=16] {'tensor'}, use_global_device_ids=true, to_apply=%region_19.0 | all-reduce | flops 3 | bytes 24 | tf_op jit(solution)/shard_map/psum | solution.py:11
  226.9 0.6 multiply_reduce_fusion.14
  227.5 31.0 %psum.142 = f32[]{:T(128)} all-reduce(f32[]{:T(128)} %get-tuple-element.26), channel_id=1, replica_groups=mesh['dp'=16,'tensor'=16] {'tensor'}, use_global_device_ids=true, to_apply=%region_21.0 | all-reduce | flops 1 | bytes 8 | tf_op jit(solution)/shard_map/psum | solution.py:15
  259.4 28.7 %psum.143 = f32[4]{0:T(128)S(1)} all-reduce(f32[4]{0:T(128)S(1)} %convolution_bitcast_fusion.3), channel_id=1, replica_groups=mesh['dp'=16,'tensor'=16] {'tensor'}, use_global_device_ids=true, to_apply=%region_22.0 | all-reduce | flops 4 | bytes 32 | tf_op jit(solution)/shard_map/psum | solution.py:11
  288.2 0.6 multiply_reduce_fusion.13
  288.8 31.2 %psum.144 = f32[]{:T(128)} all-reduce(f32[]{:T(128)} %get-tuple-element.24), channel_id=1, replica_groups=mesh['dp'=16,'tensor'=16] {'tensor'}, use_global_device_ids=true, to_apply=%region_24.0 | all-reduce | flops 1 | bytes 8 | tf_op jit(solution)/shard_map/psum | solution.py:15
  320.9 28.9 %psum.145 = f32[5]{0:T(128)S(1)} all-reduce(f32[5]{0:T(128)S(1)} %convolution_bitcast_fusion.2), channel_id=1, replica_groups=mesh['dp'=16,'tensor'=16] {'tensor'}, use_global_device_ids=true, to_apply=%region_25.0 | all-reduce | flops 5 | bytes 40 | tf_op jit(solution)/shard_map/psum | solution.py:11
  349.9 0.6 multiply_reduce_fusion.12
  350.5 30.3 %psum.146 = f32[]{:T(128)} all-reduce(f32[]{:T(128)} %get-tuple-element.22), channel_id=1, replica_groups=mesh['dp'=16,'tensor'=16] {'tensor'}, use_global_device_ids=true, to_apply=%region_27.0 | all-reduce | flops 1 | bytes 8 | tf_op jit(solution)/shard_map/psum | solution.py:15
  381.7 28.8 %psum.147 = f32[6]{0:T(128)S(1)} all-reduce(f32[6]{0:T(128)S(1)} %convolution_bitcast_fusion.1), channel_id=1, replica_groups=mesh['dp'=16,'tensor'=16] {'tensor'}, use_global_device_ids=true, to_apply=%region_28.0 | all-reduce | flops 6 | bytes 48 | tf_op jit(solution)/shard_map/psum | solution.py:11
  410.6 0.6 multiply_reduce_fusion.11
  411.2 30.3 %psum.148 = f32[]{:T(128)} all-reduce(f32[]{:T(128)} %get-tuple-element.20), channel_id=1, replica_groups=mesh['dp'=16,'tensor'=16] {'tensor'}, use_global_device_ids=true, to_apply=%region_30.0 | all-reduce | flops 1 | bytes 8 | tf_op jit(solution)/shard_map/psum | solution.py:15
  442.4 28.8 %psum.149 = f32[7]{0:T(128)S(1)} all-reduce(f32[7]{0:T(128)S(1)} %convolution_bitcast_fusion), channel_id=1, replica_groups=mesh['dp'=16,'tensor'=16] {'tensor'}, use_global_device_ids=true, to_apply=%region_31.0 | all-reduce | flops 7 | bytes 56 | tf_op jit(solution)/shard_map/psum | solution.py:11
  471.3 0.6 multiply_reduce_fusion.10
  471.9 30.4 %psum.150 = f32[]{:T(128)} all-reduce(f32[]{:T(128)} %get-tuple-element.18), channel_id=1, replica_groups=mesh['dp'=16,'tensor'=16] {'tensor'}, use_global_device_ids=true, to_apply=%region_33.0 | all-reduce | flops 1 | bytes 8 | tf_op jit(solution)/shard_map/psum | solution.py:15
  503.0 3.6 fusion.24
  506.7 1.4 fusion.27
  508.1 349.0 %all-reduce.3.cloned.1.call-done = (f32[8192,8]{0,1:T(8,128)}, f32[4096,8]{0,1:T(8,128)}) async-done(((f32[8192,8]{0,1:T(8,128)}, f32[4096,8]{0,1:T(8,128)}), (f32[8192,8]{0,1:T(8,128)}, f32[4096,8]{0,1:T(8,128)})) %all-reduce.3.cloned.1.call-update) | async-done | bytes 393232 | tf_op jit(solution)/shard_map/psum | solution.py:71
  857.1 1.7 multiply_reduce_fusion.8
  859.5 0.9 broadcast_multiply_fusion
  860.4 2.3 fusion.67
  863.3 1.3 multiply_reduce_fusion.7
  865.2 0.7 broadcast_multiply_fusion.7
  865.9 0.7 convolution_bitcast_fusion.11
  867.0 0.6 multiply_reduce_fusion.6
  868.3 1.6 convolution_bitcast_fusion.10
  870.4 0.6 multiply_reduce_fusion.5
  871.7 0.7 convolution_bitcast_fusion.9
  872.9 0.6 multiply_reduce_fusion.4
  874.5 0.7 convolution_bitcast_fusion.8
  875.5 0.6 multiply_reduce_fusion.3
  877.2 0.7 convolution_bitcast_fusion.7
  879.9 0.7 convolution_bitcast_fusion.6
  881.0 0.6 multiply_reduce_fusion.1
  882.7 2.2 fusion.11
  884.9 23.4 %psum.134 = f32[128,8]{0,1:T(8,128)S(1)} all-reduce(f32[128,8]{0,1:T(8,128)S(1)} %fusion.11), channel_id=1, replica_groups=mesh['dp'=16,'tensor'=16] {'dp'}, use_global_device_ids=true, to_apply=%region_9.0 | all-reduce | flops 1024 | bytes 8192 | tf_op jit(solution)/shard_map/psum | solution.py:87
  908.3 9.3 fusion.1
  917.6 5.0 fusion.3
  (62 shorter events, 8.0 us)
Async XLA Ops:
  7.2 849.9 %all-reduce.3.cloned.1.call-start = ((), (), s32[]{:S(2)}) async-start(), calls=%async_computation | async-start | bytes 786432 | tf_op jit(solution)/shard_map/psum | solution.py:71
  503.0 3.7 copy-start
  503.0 3.6 copy-start.1
  503.0 3.6 copy-start.7
  857.1 14.6 %copy-start.4 = (f32[8192,8]{0,1:T(8,128)S(1)}, f32[8192,8]{0,1:T(8,128)}, u32[]{:S(2)}) copy-start(f32[8192,8]{0,1:T(8,128)} %get-tuple-element.4) | copy-start | bytes 786436
  860.4 57.2 %copy-start.5 = (f32[4096,8]{0,1:T(8,128)}, f32[4096,8]{0,1:T(8,128)S(1)}, u32[]{:S(2)}) copy-start(f32[4096,8]{0,1:T(8,128)S(1)} %broadcast_multiply_fusion) | copy-start | bytes 393220
  908.2 9.3 %copy-start.6 = (f32[128,8]{0,1:T(8,128)}, f32[128,8]{0,1:T(8,128)S(1)}, u32[]{:S(2)}) copy-start(f32[128,8]{0,1:T(8,128)S(1)} %broadcast_multiply_fusion.8) | copy-start | bytes 12292
  908.3 9.3 copy-start.2
  908.3 9.3 copy-start.3
Sparse Core Ops, SparseCore 0:
  508.2 348.7 all-reduce.2
where the time goes:
time: 931 us; the launch traced here: 929 us
  blocking collectives  502 us (54%)
  waiting for transfers between devices  349 us (37%)
  matrix products  33.4 us (4%)
  between operations  25.4 us (3%)
  other arithmetic  17.9 us (2%)
    psum x1, waiting for transfers between devices, per_device(): sketch_kv = lax.psum(partial_kv, ('dp', 'tensor'))  349 us
    psum x8, blocking collectives, length_total(): return lax.psum(values, 'tensor')  249 us
    psum x7, blocking collectives, projection_total(): return lax.psum(values, 'tensor')  201 us
    psum x1, blocking collectives, per_device(): sketch_out = lax.psum(partial_out, 'dp')  27.9 us
    psum x1, blocking collectives, per_device(): factor_kv = lax.psum(term_kv, 'dp') / replicas  23.4 us
  transfers between devices with their start and end apart: 1, of which 1 were waited for; matrix products, arithmetic and copies ran while one was open for 0% of the time, Pallas kernels for 0%

commit v1 on v0

v1 whole, which is shorter than its diff:
```python
import jax
import jax.numpy as jnp
from jax import lax
from jax.experimental import pallas as pl
from jax.experimental.pallas import tpu as pltpu
from jax.sharding import PartitionSpec as P

epsilon = 1e-06
f32 = jnp.float32
bf16 = jnp.bfloat16
LANES = 128
KV_CHUNKS = 8
OUT_CHUNKS = 8
limit = pltpu.CompilerParams(vmem_limit_bytes=24 * 1024 * 1024)
whole = pl.BlockSpec(memory_space=pltpu.VMEM)


def resident(value):
    return pltpu.with_memory_space_constraint(value, pltpu.VMEM)


def distant(value):
    return pltpu.with_memory_space_constraint(value, pltpu.HBM)


def merge(grad, error):
    return (grad.astype(f32) + error.astype(f32)).astype(bf16)


def split(value):
    high = value.astype(bf16)
    low = (value - high.astype(f32)).astype(bf16)
    return high, low


def row(tile, index):
    return jnp.broadcast_to(tile[index : index + 1, :], tile.shape)


def gram_columns(tiles):
    sums = [None] * 8
    for tile in tiles:
        for j in range(8):
            product = tile * row(tile, j)
            sums[j] = product if sums[j] is None else sums[j] + product
    return [
        jnp.broadcast_to(jnp.sum(total, axis=1, keepdims=True), (8, LANES)) for total in sums
    ]


def cholesky(columns):
    place = lax.broadcasted_iota(jnp.int32, (8, LANES), 0)
    columns = [
        column + jnp.where(place == j, epsilon, 0.0).astype(f32)
        for j, column in enumerate(columns)
    ]
    steps = []
    scale = jnp.zeros((8, LANES), f32)
    for j in range(8):
        inverse = lax.rsqrt(jnp.maximum(row(columns[j], j), epsilon))
        lower = jnp.where(place > j, columns[j] * inverse, 0.0)
        for k in range(j + 1, 8):
            columns[k] = columns[k] - lower * row(lower, k)
        steps.append(lower * inverse)
        scale = jnp.where(place == j, inverse, scale)
    return steps, scale


def substitute(tile, steps, scale):
    for j in range(7):
        tile = tile - steps[j] * row(tile, j)
    return tile * scale


def left_terms(value):
    high, low = split(value)
    high, low = high.astype(f32), low.astype(f32)
    return jnp.concatenate([high, low, high, jnp.zeros_like(high)], axis=0).T.astype(bf16)


def right_terms(value):
    high, low = split(value)
    high, low = high.astype(f32), low.astype(f32)
    return jnp.concatenate([high, high, low, jnp.zeros_like(high)], axis=0).astype(bf16)


def first(core, grad_kv, error_kv, grad_out, error_out, warm_kv, warm_out, merged_kv, merged_out,
          keep, give, gkv, ekv, gout, eout, arrived):
    rows = gkv.shape[0] // KV_CHUNKS
    wide = gout.shape[1] // OUT_CHUNKS
    copies = []
    for c in range(KV_CHUNKS):
        part = pl.ds(c * rows, rows)
        for k, (source, target) in enumerate(((grad_kv, gkv), (error_kv, ekv))):
            copy = pltpu.make_async_copy(source.at[part], target.at[part], arrived.at[k, c])
            copy.start()
            copies.append(copy)
    for c in range(OUT_CHUNKS):
        part = pl.ds(c * wide, wide)
        for k, (source, target) in enumerate(((grad_out, gout), (error_out, eout))):
            copy = pltpu.make_async_copy(
                source.at[:, part], target.at[:, part], arrived.at[2 + k, c]
            )
            copy.start()
            copies.append(copy)
    right = warm_kv[...].astype(bf16)
    even = jnp.full((8, LANES), core[0], jnp.int32) == 0
    for c in range(KV_CHUNKS):
        copies[2 * c].wait()
        copies[2 * c + 1].wait()
        part = pl.ds(c * rows, rows)
        merged = merge(gkv[part, :], ekv[part, :])
        merged_kv[part, :] = merged
        sketch = lax.dot_general(
            right, merged, (((1,), (1,)), ((), ())), preferred_element_type=f32
        )
        for k in range(4):
            zero = sketch[:, k * LANES : (k + 1) * LANES]
            one = sketch[:, (k + 4) * LANES : (k + 5) * LANES]
            keep[c, k] = jnp.where(even, zero, one)
            give[c, k] = jnp.where(even, one, zero)
    total = None
    for c in range(OUT_CHUNKS):
        index = 2 * KV_CHUNKS + 2 * c
        copies[index].wait()
        copies[index + 1].wait()
        part = pl.ds(c * wide, wide)
        merged = merge(gout[:, part], eout[:, part])
        merged_out[:, part] = merged
        sketch = lax.dot_general(
            warm_out[:, part].astype(bf16),
            merged,
            (((1,), (1,)), ((), ())),
            preferred_element_type=f32,
        )
        total = sketch if total is None else total + sketch
    for z in range(8):
        for k in range(2):
            tile = total[:, k * LANES : (k + 1) * LANES]
            keep[z, 4 + k] = tile
            give[z, 4 + k] = tile


def total_of(received, index):
    value = received[0, index]
    for d in range(1, received.shape[0]):
        value = value + received[d, index]
    return value


def second(received, merged_out, send, sketch_out):
    tiles = [total_of(received, k) for k in range(6)]
    sketch_out[0] = tiles[4]
    sketch_out[1] = tiles[5]
    gram = jnp.zeros((8, LANES), f32)
    lane = lax.broadcasted_iota(jnp.int32, (8, LANES), 1)
    for j, column in enumerate(gram_columns(tiles[4:6])):
        gram = jnp.where(lane == j, column, gram)
    high, low = split(jnp.concatenate(tiles[4:6], axis=1))
    left = jnp.concatenate([high.astype(f32), low.astype(f32)], axis=0).astype(bf16)
    for c in range(4):
        both = jnp.dot(left, merged_out[:, c * 1024 : (c + 1) * 1024], preferred_element_type=f32)
        both = both[:8] + both[8:]
        for k in range(8):
            tile = 8 * c + k
            send[tile // 2, 4 + tile % 2] = both[:, k * LANES : (k + 1) * LANES]
    for d in range(16):
        for k in range(4):
            send[d, k] = tiles[k]
        send[d, 6] = gram


def third(received, send, gram):
    tiles = [total_of(received, k) for k in range(7)]
    for z in range(8):
        for k in range(6):
            send[z, k] = tiles[k]
    gram[...] = tiles[6]


def fourth_out(mine, other, send):
    for k in range(2):
        value = total_of(mine, 4 + k) + total_of(other, 4 + k)
        for d in range(16):
            send[d, k] = value


def fourth_kv(core, mine, other, merged_kv, send, basis):
    even = jnp.full((8, LANES), core[0], jnp.int32) == 0
    tiles = []
    for z in range(8):
        for k in range(4):
            tiles.append(jnp.where(even, mine[z, k], other[z, k]))
        for k in range(4):
            tiles.append(jnp.where(even, other[z, k], mine[z, k]))
    steps, scale = cholesky(gram_columns(tiles))
    term = jnp.zeros((8, LANES), f32)
    for c in range(8):
        done = []
        for k in range(8):
            value = substitute(tiles[8 * c + k], steps, scale)
            basis[:, (8 * c + k) * LANES : (8 * c + k + 1) * LANES] = value
            done.append(value)
        low = jnp.concatenate(done, axis=1).astype(bf16)
        term = term + jnp.dot(
            low, merged_kv[c * 1024 : (c + 1) * 1024, :], preferred_element_type=f32
        )
    for d in range(16):
        send[d] = term


def finish_out(received, gram, sketch_out, merged_out, factor, residual, done, sent):
    lane = lax.broadcasted_iota(jnp.int32, (8, LANES), 1)
    columns = [
        jnp.broadcast_to(
            jnp.sum(jnp.where(lane == j, gram[...], 0.0), axis=1, keepdims=True), (8, LANES)
        )
        for j in range(8)
    ]
    steps, scale = cholesky(columns)
    basis = [substitute(sketch_out[k], steps, scale) for k in range(2)]
    left = left_terms(jnp.concatenate(basis, axis=1))
    copies = []
    wide = 1024
    for c in range(4):
        values = []
        for k in range(8):
            tile = 8 * c + k
            value = substitute(received[tile // 2, tile % 2], steps, scale) * (1.0 / 16.0)
            factor[:, tile * LANES : (tile + 1) * LANES] = value
            values.append(value)
        right = right_terms(jnp.concatenate(values, axis=1))
        part = pl.ds(c * wide, wide)
        approx = jnp.dot(left, right, preferred_element_type=f32)
        done[:, part] = (merged_out[:, part].astype(f32) - approx).astype(bf16)
        copy = pltpu.make_async_copy(done.at[:, part], residual.at[:, part], sent.at[c])
        copy.start()
        copies.append(copy)
    for copy in copies:
        copy.wait()


def finish_kv(received, basis, merged_kv, factor, residual, done, sent):
    value = received[0]
    for d in range(1, 16):
        value = value + received[d]
    value = value * (1.0 / 16.0)
    factor[...] = value
    right = right_terms(value)
    copies = []
    rows = 1024
    for c in range(8):
        part = pl.ds(c * rows, rows)
        left = left_terms(basis[:, part])
        approx = jnp.dot(left, right, preferred_element_type=f32)
        done[part, :] = (merged_kv[part, :].astype(f32) - approx).astype(bf16)
        copy = pltpu.make_async_copy(done.at[part], residual.at[part], sent.at[c])
        copy.start()
        copies.append(copy)
    for copy in copies:
        copy.wait()


def exchange(value, axis, groups=None):
    return lax.all_to_all(value, axis, 0, 0, axis_index_groups=groups)


def per_device(grad_kv, error_kv, grad_out, error_out, warm_kv, warm_out):
    grad_kv, error_kv, grad_out, error_out = (
        value[0] for value in (grad_kv, error_kv, grad_out, error_out)
    )
    kv_shape, out_shape = grad_kv.shape, grad_out.shape
    far = pl.BlockSpec(memory_space=pltpu.HBM)
    scalar = pl.BlockSpec(memory_space=pltpu.SMEM)
    columns = [[2 * z + c for z in range(8)] for c in range(2)]
    swap = [(d, d ^ 1) for d in range(16)]
    core = (lax.axis_index("dp") % 2).astype(jnp.int32).reshape(1)
    merged_kv, merged_out, keep, give = pl.pallas_call(
        first,
        out_shape=(
            pltpu.VMEM(kv_shape, bf16),
            pltpu.VMEM(out_shape, bf16),
            pltpu.VMEM((8, 6, 8, LANES), f32),
            pltpu.VMEM((8, 6, 8, LANES), f32),
        ),
        in_specs=[scalar] + [far] * 4 + [whole] * 2,
        out_specs=(whole,) * 4,
        scratch_shapes=[
            pltpu.VMEM(kv_shape, bf16),
            pltpu.VMEM(kv_shape, bf16),
            pltpu.VMEM(out_shape, bf16),
            pltpu.VMEM(out_shape, bf16),
            pltpu.SemaphoreType.DMA((4, 8)),
        ],
        compiler_params=limit,
        name="first",
    )(core, *(distant(v) for v in (grad_kv, error_kv, grad_out, error_out)), warm_kv.T, warm_out.T)

    received = exchange(keep + lax.ppermute(give, "dp", swap), "dp", columns)
    send, sketch_out = pl.pallas_call(
        second,
        out_shape=(pltpu.VMEM((16, 7, 8, LANES), f32), pltpu.VMEM((2, 8, LANES), f32)),
        in_specs=[whole] * 2,
        out_specs=(whole,) * 2,
        compiler_params=limit,
        name="second",
    )(resident(received), resident(merged_out))

    received = exchange(send, "tensor")
    send, gram = pl.pallas_call(
        third,
        out_shape=(pltpu.VMEM((8, 6, 8, LANES), f32), pltpu.VMEM((8, LANES), f32)),
        in_specs=[whole],
        out_specs=(whole,) * 2,
        compiler_params=limit,
        name="third",
    )(resident(received))

    mine = exchange(send, "dp", columns)
    other = lax.ppermute(mine, "dp", swap)
    send_out = pl.pallas_call(
        fourth_out,
        out_shape=pltpu.VMEM((16, 2, 8, LANES), f32),
        in_specs=[whole] * 2,
        out_specs=whole,
        compiler_params=limit,
        name="fourth_out",
    )(resident(mine), resident(other))
    received_out = exchange(send_out, "tensor")

    send_kv, basis = pl.pallas_call(
        fourth_kv,
        out_shape=(pltpu.VMEM((16, 8, LANES), f32), pltpu.VMEM((8, kv_shape[0]), f32)),
        in_specs=[scalar] + [whole] * 3,
        out_specs=(whole,) * 2,
        compiler_params=limit,
        name="fourth_kv",
    )(core, resident(mine), resident(other), resident(merged_kv))
    received_kv = exchange(send_kv, "dp")

    factor_out, residual_out = pl.pallas_call(
        finish_out,
        out_shape=(
            jax.ShapeDtypeStruct((8, out_shape[1]), f32),
            pltpu.HBM(out_shape, bf16),
        ),
        in_specs=[whole] * 4,
        out_specs=(whole, far),
        scratch_shapes=[pltpu.VMEM(out_shape, bf16), pltpu.SemaphoreType.DMA((4,))],
        compiler_params=limit,
        name="finish_out",
    )(resident(received_out), resident(gram), resident(sketch_out), resident(merged_out))

    factor_kv, residual_kv = pl.pallas_call(
        finish_kv,
        out_shape=(
            jax.ShapeDtypeStruct((8, kv_shape[1]), f32),
            pltpu.HBM(kv_shape, bf16),
        ),
        in_specs=[whole] * 3,
        out_specs=(whole, far),
        scratch_shapes=[pltpu.VMEM(kv_shape, bf16), pltpu.SemaphoreType.DMA((8,))],
        compiler_params=limit,
        name="finish_kv",
    )(resident(received_kv), resident(basis), resident(merged_kv))

    return factor_kv.T, factor_out.T, residual_kv[None], residual_out[None]


def solution(mesh):
    placed = (
        P("dp", None, "tensor"),
        P("dp", None, "tensor"),
        P("dp", "tensor", None),
        P("dp", "tensor", None),
        P("tensor", None),
        P(),
    )
    return jax.shard_map(
        per_device,
        mesh=mesh,
        in_specs=placed,
        out_specs=(P("tensor", None), P(), P("dp", None, "tensor"), P("dp", "tensor", None)),
        check_vma=False,
    )
```

time: 931 us -> 85.2 us (0.09)
  blocking collectives: 502 us -> 43.2 us
  waiting for transfers between devices: 349 us -> 12.1 us
  matrix products: 33.4 us -> 0 us
  between operations: 25.4 us -> 0.71 us
  other arithmetic: 17.9 us -> 0.02 us
  starting transfers between devices: 0.04 us -> 14 us
  Pallas kernels: 0 us -> 11.6 us
    psum x17 -> x0, blocking collectives: 502 us -> none  [the longest x8 249 us: length_total(): return lax.psum(values, 'tensor')]
    psum x1 -> x0, waiting for transfers between devices: 349 us -> none  [per_device(): sketch_kv = lax.psum(partial_kv, ('dp', 'tensor'))]
    all_to_all x0 -> x3, blocking collectives: none -> 43.2 us  [exchange(): return lax.all_to_all(value, axis, 0, 0, axis_index_groups=groups)]
    dot_general x30 -> x0, matrix products: 33.4 us -> none  [the longest x1 9.26 us: per_device(): jnp.dot(basis_kv, factor_kv.T, precision=highest, preferred_element_type=...]
    reduce_sum x16 -> x0, other arithmetic: 12.1 us -> none  [orthonormal(): squares = tuple((jnp.sum(vector * vector) for vector in vectors))]
    pallas_call x0 -> x7, Pallas kernels: none -> 11.6 us  [the longest x1 4.3 us: per_device(): pl.pallas_call(first, out_shape=(pltpu.VMEM(kv_shape, bf16), pltpu.VMEM(o...]
    all_to_all x0 -> x2, waiting for transfers between devices: none -> 9.92 us  [exchange(): return lax.all_to_all(value, axis, 0, 0, axis_index_groups=groups)]
  transfers between devices with their start and end apart: 1 -> 4, of which waited for: 1 -> 4; matrix products, arithmetic and copies ran while one was open for 0% -> 0% of each run, Pallas kernels for 0% -> 4%
where the time goes in v1:
time: 85.2 us; the launch traced here: 84.8 us
  blocking collectives  43.2 us (51%)
  starting transfers between devices  14 us (16%)
  waiting for transfers between devices  12.1 us (14%)
  Pallas kernels  11.6 us (14%)
  local copies, waits for them, and re-layouts  3.18 us (4%)
    all_to_all x3, blocking collectives, exchange(): return lax.all_to_all(value, axis, 0, 0, axis_index_groups=groups)  43.2 us
    all_to_all x2, waiting for transfers between devices, exchange(): return lax.all_to_all(value, axis, 0, 0, axis_index_groups=groups)  9.92 us
    all_to_all x2, starting transfers between devices, exchange(): return lax.all_to_all(value, axis, 0, 0, axis_index_groups=groups)  7.18 us
    pallas_call x1, Pallas kernels, per_device(): pl.pallas_call(first, out_shape=(pltpu.VMEM(kv_shape, bf16), pltpu.VMEM(o...  4.3 us
    ppermute x1, starting transfers between devices, per_device(): other = lax.ppermute(mine, 'dp', swap)  3.53 us
    ppermute x1, starting transfers between devices, per_device(): received = exchange(keep + lax.ppermute(give, 'dp', swap), 'dp', columns)  3.33 us
    unnamed x8, local copies, waits for them, and re-layouts  3.18 us
    pallas_call x1, Pallas kernels, per_device(): pl.pallas_call(finish_out, out_shape=(jax.ShapeDtypeStruct((8, out_shape[...  2.51 us
  transfers between devices with their start and end apart: 4, of which 4 were waited for; matrix products, arithmetic and copies ran while one was open for 0% of the time, Pallas kernels for 4%

profile of v1, /device:TPU:1, one launch (start us, length us, event | category | flops | bytes accessed | tf_op | source)
XLA Modules:
  0.0 84.8 jit_solution(2457446901877069407)
XLA Ops:
  0.6 0.0 copy-start.2
  0.7 0.9 %copy-done.2 = f32[4096,8]{0,1:T(8,128)S(1)} copy-done((f32[4096,8]{0,1:T(8,128)S(1)}, f32[4096,8]{0,1:T(8,128)}, u32[]{:S(2)}) %copy-start.2) | copy-done | bytes 131096
  1.5 0.0 copy-start.3
  1.6 0.7 copy-done.3
  2.2 4.3 %first.1 = (bf16[8192,128]{1,0:T(8,128)(2,1)S(1)}, bf16[256,4096]{1,0:T(8,128)(2,1)S(1)}, f32[8,6,8,128]{3,2,1,0:T(8,128)S(1)}, f32[8,6,8,128]{3,2,1,0:T(8,128)S(1)}) custom-call(s32[1]{0:T(128)} %bitcast.core, bf16[8192,128]{1,0:T(8,128)(2,1)} %bitcast.13, bf16[8192,128]{1,0:T(8,128)(2,1)} %bitcast.14, bf16[256,4096]{1,0:T(8,128)(2,1)} %bitcast.15, ...), custom_call_target="tpu_custom_call" | custom-call | tf_op jit(solution)/shard_map/first/pallas_call | solution.py:278
  6.5 0.0 copy-start
  6.6 3.3 %collective-permute-start = (f32[8,6,8,128]{3,2,1,0:T(8,128)S(1)}, f32[8,6,8,128]{3,2,1,0:T(8,128)S(1)}, u32[]{:S(2)}, u32[]{:S(2)}) collective-permute-start(f32[8,6,8,128]{3,2,1,0:T(8,128)S(1)} %get-tuple-element.19), channel_id=1, source_target_pairs={{0,16},{16,0},{32,48},{48,32},{64,80},{80,64},{96,112},{112,96},{1... | collective-permute-start | bytes 589832 | tf_op jit(solution)/shard_map/ppermute | solution.py:299
  9.9 1.1 %collective-permute-done = f32[8,6,8,128]{3,2,1,0:T(8,128)S(1)} collective-permute-done((f32[8,6,8,128]{3,2,1,0:T(8,128)S(1)}, f32[8,6,8,128]{3,2,1,0:T(8,128)S(1)}, u32[]{:S(2)}, u32[]{:S(2)}) %collective-permute-start) | collective-permute-done | bytes 196640 | tf_op jit(solution)/shard_map/ppermute | solution.py:299
  11.0 15.7 %all_to_all.25.received = f32[8,6,8,128]{3,2,1,0:T(8,128)S(1)} all-to-all(f32[8,6,8,128]{3,2,1,0:T(8,128)S(1)} %add.8), channel_id=1, replica_groups={{0,32,64,96,128,160,192,224},{16,48,80,112,144,176,208,240},{1,33,65,97..., dimensions={0} | all-to-all | bytes 393216 | tf_op jit(solution)/shard_map/all_to_all | solution.py:265
  26.7 0.4 second.1
  27.0 15.5 %all_to_all.26.received = f32[16,7,8,128]{3,2,1,0:T(8,128)S(1)} all-to-all(f32[16,7,8,128]{3,2,1,0:T(8,128)S(1)} %get-tuple-element.21), channel_id=1, replica_groups=mesh['dp'=16,'tensor'=16] {'tensor'}, dimensions={0} | all-to-all | bytes 917504 | tf_op jit(solution)/shard_map/all_to_all | solution.py:265
  42.5 12.0 %all_to_all.27.mine = f32[8,6,8,128]{3,2,1,0:T(8,128)S(1)} all-to-all(f32[8,6,8,128]{3,2,1,0:T(8,128)S(1)} %get-tuple-element.22), channel_id=1, replica_groups={{0,32,64,96,128,160,192,224},{16,48,80,112,144,176,208,240},{1,33,65,97..., dimensions={0} | all-to-all | bytes 393216 | tf_op jit(solution)/shard_map/all_to_all | solution.py:265
  54.6 3.5 %collective-permute-start.1 = (f32[8,6,8,128]{3,2,1,0:T(8,128)S(1)}, f32[8,6,8,128]{3,2,1,0:T(8,128)S(1)}, u32[]{:S(2)}, u32[]{:S(2)}) collective-permute-start(f32[8,6,8,128]{3,2,1,0:T(8,128)S(1)} %all_to_all.27.mine), channel_id=1, source_target_pairs={{0,16},{16,0},{32,48},{48,32},{64,80},{80,64},{96,112},{112,96},{1... | collective-permute-start | bytes 589832 | tf_op jit(solution)/shard_map/ppermute | solution.py:320
  58.1 1.1 %collective-permute-done.1.other = f32[8,6,8,128]{3,2,1,0:T(8,128)S(1)} collective-permute-done((f32[8,6,8,128]{3,2,1,0:T(8,128)S(1)}, f32[8,6,8,128]{3,2,1,0:T(8,128)S(1)}, u32[]{:S(2)}, u32[]{:S(2)}) %collective-permute-start.1) | collective-permute-done | bytes 196640 | tf_op jit(solution)/shard_map/ppermute | solution.py:320
  59.2 0.0 copy-done
  59.2 1.4 %fourth_kv.1 = (f32[16,8,128]{2,1,0:T(8,128)}, f32[8,8192]{1,0:T(8,128)S(1)}) custom-call(s32[1]{0:T(128)} %bitcast.core, f32[8,6,8,128]{3,2,1,0:T(8,128)S(1)} %all_to_all.27.mine, f32[8,6,8,128]{3,2,1,0:T(8,128)S(1)} %collective-permute-done.1.other, bf16[8192,128]{1,0:T(8,128)(2,1)S(1)} %get-tuple-element.23.merged_kv), custom_call_target="tpu_custom_call" | custom-call | tf_op jit(solution)/shard_map/fourth_kv/pallas_call | solution.py:331
  60.5 3.7 %all-to-all-start.3 = ((f32[16,8,128]{2,1,0:T(8,128)}), f32[16,8,128]{2,1,0:T(8,128)S(1)}, u32[]{:S(2)}, u32[]{:S(2)}) async-start(f32[16,8,128]{2,1,0:T(8,128)} %get-tuple-element.24), calls=%async_computation.3 | async-start | bytes 131072 | tf_op jit(solution)/shard_map/all_to_all | solution.py:265
  64.2 0.7 fourth_out.1
  64.9 7.2 %all-to-all-done.3.received = f32[16,8,128]{2,1,0:T(8,128)S(1)} async-done(((f32[16,8,128]{2,1,0:T(8,128)}), f32[16,8,128]{2,1,0:T(8,128)S(1)}, u32[]{:S(2)}, u32[]{:S(2)}) %all-to-all-start.3) | async-done | bytes 65568 | tf_op jit(solution)/shard_map/all_to_all | solution.py:265
  72.0 3.5 %all-to-all-start.4 = ((f32[16,2,8,128]{3,2,1,0:T(8,128)}), f32[16,2,8,128]{3,2,1,0:T(8,128)S(1)}, u32[]{:S(2)}, u32[]{:S(2)}) async-start(f32[16,2,8,128]{3,2,1,0:T(8,128)} %fourth_out.1), calls=%async_computation.4 | async-start | bytes 262144 | tf_op jit(solution)/shard_map/all_to_all | solution.py:265
  75.6 0.0 copy-start.1
  75.6 1.6 %copy-done.1 = bf16[8192,128]{1,0:T(8,128)(2,1)S(1)} copy-done((bf16[8192,128]{1,0:T(8,128)(2,1)S(1)}, bf16[8192,128]{1,0:T(8,128)(2,1)}, u32[]{:S(2)}) %copy-start.1) | copy-done | bytes 2097176
  77.2 2.4 %finish_kv.1 = (f32[8,128]{1,0:T(8,128)}, bf16[8192,128]{1,0:T(8,128)(2,1)}) custom-call(f32[16,8,128]{2,1,0:T(8,128)S(1)} %all-to-all-done.3.received, f32[8,8192]{1,0:T(8,128)S(1)} %get-tuple-element.25.basis, bf16[8192,128]{1,0:T(8,128)(2,1)S(1)} %copy-done.1), custom_call_target="tpu_custom_call" | custom-call | tf_op jit(solution)/shard_map/finish_kv/pallas_call | solution.py:354
  79.5 2.8 %all-to-all-done.4.received = f32[16,2,8,128]{3,2,1,0:T(8,128)S(1)} async-done(((f32[16,2,8,128]{3,2,1,0:T(8,128)}), f32[16,2,8,128]{3,2,1,0:T(8,128)S(1)}, u32[]{:S(2)}, u32[]{:S(2)}) %all-to-all-start.4) | async-done | bytes 131104 | tf_op jit(solution)/shard_map/all_to_all | solution.py:265
  82.3 2.5 %finish_out.1 = (f32[8,4096]{1,0:T(8,128)}, bf16[256,4096]{1,0:T(8,128)(2,1)}) custom-call(f32[16,2,8,128]{3,2,1,0:T(8,128)S(1)} %all-to-all-done.4.received, f32[8,128]{1,0:T(8,128)S(1)} %get-tuple-element.27.gram, f32[2,8,128]{2,1,0:T(8,128)S(1)} %get-tuple-element.28.sketch_out, bf16[256,4096]{1,0:T(8,128)(2,1)S(1)} %get-tuple-element.20.merged_out), custom_call_target="tpu_custom_call" | custom-call | tf_op jit(solution)/shard_map/finish_out/pallas_call | solution.py:341
  (2 shorter events, 0.1 us)
Async XLA Ops:
  0.6 0.9 %copy-start.2 = (f32[4096,8]{0,1:T(8,128)S(1)}, f32[4096,8]{0,1:T(8,128)}, u32[]{:S(2)}) copy-start(f32[4096,8]{0,1:T(8,128)} %param.11) | copy-start | bytes 393220
  1.5 0.7 copy-start.3
  6.5 52.6 %copy-start = (bf16[8192,128]{1,0:T(8,128)(2,1)}, bf16[8192,128]{1,0:T(8,128)(2,1)S(1)}, u32[]{:S(2)}) copy-start(bf16[8192,128]{1,0:T(8,128)(2,1)S(1)} %get-tuple-element.23.merged_kv) | copy-start | bytes 6291460
  6.6 4.4 %collective-permute-start = (f32[8,6,8,128]{3,2,1,0:T(8,128)S(1)}, f32[8,6,8,128]{3,2,1,0:T(8,128)S(1)}, u32[]{:S(2)}, u32[]{:S(2)}) collective-permute-start(f32[8,6,8,128]{3,2,1,0:T(8,128)S(1)} %get-tuple-element.19), channel_id=1, source_target_pairs={{0,16},{16,0},{32,48},{48,32},{64,80},{80,64},{96,112},{112,96},{1... | collective-permute-start | bytes 589832 | tf_op jit(solution)/shard_map/ppermute | solution.py:299
  54.6 4.6 %collective-permute-start.1 = (f32[8,6,8,128]{3,2,1,0:T(8,128)S(1)}, f32[8,6,8,128]{3,2,1,0:T(8,128)S(1)}, u32[]{:S(2)}, u32[]{:S(2)}) collective-permute-start(f32[8,6,8,128]{3,2,1,0:T(8,128)S(1)} %all_to_all.27.mine), channel_id=1, source_target_pairs={{0,16},{16,0},{32,48},{48,32},{64,80},{80,64},{96,112},{112,96},{1... | collective-permute-start | bytes 589832 | tf_op jit(solution)/shard_map/ppermute | solution.py:320
  60.5 11.5 %all-to-all-start.3 = ((f32[16,8,128]{2,1,0:T(8,128)}), f32[16,8,128]{2,1,0:T(8,128)S(1)}, u32[]{:S(2)}, u32[]{:S(2)}) async-start(f32[16,8,128]{2,1,0:T(8,128)} %get-tuple-element.24), calls=%async_computation.3 | async-start | bytes 131072 | tf_op jit(solution)/shard_map/all_to_all | solution.py:265
  72.0 10.2 %all-to-all-start.4 = ((f32[16,2,8,128]{3,2,1,0:T(8,128)}), f32[16,2,8,128]{3,2,1,0:T(8,128)S(1)}, u32[]{:S(2)}, u32[]{:S(2)}) async-start(f32[16,2,8,128]{3,2,1,0:T(8,128)} %fourth_out.1), calls=%async_computation.4 | async-start | bytes 262144 | tf_op jit(solution)/shard_map/all_to_all | solution.py:265
  75.6 1.6 %copy-start.1 = (bf16[8192,128]{1,0:T(8,128)(2,1)S(1)}, bf16[8192,128]{1,0:T(8,128)(2,1)}, u32[]{:S(2)}) copy-start(bf16[8192,128]{1,0:T(8,128)(2,1)} %copy-done) | copy-start | bytes 6291460

commit v2 on v0

v2 whole, which is shorter than its diff:
```python
import jax
import jax.numpy as jnp
from jax import lax
from jax.experimental import pallas as pl
from jax.experimental.pallas import tpu as pltpu
from jax.sharding import PartitionSpec as P

epsilon = 1e-06
f32 = jnp.float32
bf16 = jnp.bfloat16
LANES = 128
KV_CHUNKS = 4
OUT_CHUNKS = 4
limit = pltpu.CompilerParams(vmem_limit_bytes=24 * 1024 * 1024)
whole = pl.BlockSpec(memory_space=pltpu.VMEM)


def resident(value):
    return pltpu.with_memory_space_constraint(value, pltpu.VMEM)


def distant(value):
    return pltpu.with_memory_space_constraint(value, pltpu.HBM)


def merge(grad, error):
    return (grad.astype(f32) + error.astype(f32)).astype(bf16)


def split(value):
    high = value.astype(bf16)
    low = (value - high.astype(f32)).astype(bf16)
    return high, low


def row(tile, index):
    return jnp.broadcast_to(tile[index : index + 1, :], tile.shape)


def gram_columns(tiles):
    sums = [None] * 8
    for tile in tiles:
        for j in range(8):
            product = tile * row(tile, j)
            sums[j] = product if sums[j] is None else sums[j] + product
    return [
        jnp.broadcast_to(jnp.sum(total, axis=1, keepdims=True), (8, LANES)) for total in sums
    ]


def cholesky(columns):
    place = lax.broadcasted_iota(jnp.int32, (8, LANES), 0)
    columns = [
        column + jnp.where(place == j, epsilon, 0.0).astype(f32)
        for j, column in enumerate(columns)
    ]
    steps = []
    scale = jnp.zeros((8, LANES), f32)
    for j in range(8):
        inverse = lax.rsqrt(jnp.maximum(row(columns[j], j), epsilon))
        lower = jnp.where(place > j, columns[j] * inverse, 0.0)
        for k in range(j + 1, 8):
            columns[k] = columns[k] - lower * row(lower, k)
        steps.append(lower * inverse)
        scale = jnp.where(place == j, inverse, scale)
    return steps, scale


def substitute(tile, steps, scale):
    for j in range(7):
        tile = tile - steps[j] * row(tile, j)
    return tile * scale


def left_terms(value):
    high, low = split(value)
    high, low = high.astype(f32), low.astype(f32)
    return jnp.concatenate([high, low, high, jnp.zeros_like(high)], axis=0).T.astype(bf16)


def right_terms(value):
    high, low = split(value)
    high, low = high.astype(f32), low.astype(f32)
    return jnp.concatenate([high, high, low, jnp.zeros_like(high)], axis=0).astype(bf16)


def block(index, size):
    start = index * size
    return pl.ds(start if isinstance(index, int) else pl.multiple_of(start, size), size)


def first_out(grad, error, warm, merged_out, send, warm_near, near, far_, arrived, warm_arrived):
    wide = near.shape[1] // OUT_CHUNKS

    def copies(c):
        part = block(c, wide)
        return [
            pltpu.make_async_copy(source.at[:, part], target.at[:, part], arrived.at[k, c])
            for k, (source, target) in enumerate(((grad, near), (error, far_)))
        ]

    warm_copy = pltpu.make_async_copy(warm, warm_near, warm_arrived)
    warm_copy.start()

    @pl.loop(0, OUT_CHUNKS)
    def _(c):
        for copy in copies(c):
            copy.start()

    warm_copy.wait()

    def step(c, total):
        for copy in copies(c):
            copy.wait()
        part = block(c, wide)
        merged = merge(near[:, part], far_[:, part])
        merged_out[:, part] = merged
        return total + lax.dot_general(
            warm_near[:, part].astype(bf16),
            merged,
            (((1,), (1,)), ((), ())),
            preferred_element_type=f32,
        )

    total = lax.fori_loop(0, OUT_CHUNKS, step, jnp.zeros((8, near.shape[0]), f32))
    for d in range(16):
        for k in range(2):
            send[d, k] = total[:, k * LANES : (k + 1) * LANES]


def first_kv(core, grad, error, warm, merged_out, merged_kv, stored_out, keep, give, warm_near,
             near, far_, done, arrived, sent, warm_arrived, out_sent):
    rows = near.shape[0] // KV_CHUNKS

    def copies(c):
        part = block(c, rows)
        return [
            pltpu.make_async_copy(source.at[part], target.at[part], arrived.at[k, c])
            for k, (source, target) in enumerate(((grad, near), (error, far_)))
        ]

    def leaving(c):
        part = block(c, rows)
        return pltpu.make_async_copy(done.at[part], merged_kv.at[part], sent.at[c])

    warm_copy = pltpu.make_async_copy(warm, warm_near, warm_arrived)
    warm_copy.start()

    @pl.loop(0, KV_CHUNKS)
    def _(c):
        for copy in copies(c):
            copy.start()

    warm_copy.wait()
    out_copy = pltpu.make_async_copy(merged_out, stored_out, out_sent)
    out_copy.start()
    right = warm_near[...].astype(bf16)
    even = jnp.full((8, LANES), core[0], jnp.int32) == 0
    for c in range(KV_CHUNKS):
        for copy in copies(c):
            copy.wait()
        part = block(c, rows)
        merged = merge(near[part, :], far_[part, :])
        done[part, :] = merged
        leaving(c).start()
        sketch = lax.dot_general(
            right, merged, (((1,), (1,)), ((), ())), preferred_element_type=f32
        )
        for t in range(4):
            for k in range(2):
                first = (4 * t + k) * LANES
                zero = sketch[:, first : first + LANES]
                one = sketch[:, first + 2 * LANES : first + 3 * LANES]
                keep[4 * c + t, k] = jnp.where(even, zero, one)
                give[4 * c + t, k] = jnp.where(even, one, zero)

    out_copy.wait()

    @pl.loop(0, KV_CHUNKS)
    def _(c):
        leaving(c).wait()


def total_of(received, index):
    value = received[0, index]
    for d in range(1, received.shape[0]):
        value = value + received[d, index]
    return value


def second(core, received, merged_out, merged_kv, keep, give, sketch_out, same_kv):
    del merged_kv, same_kv
    tiles = [total_of(received, k) for k in range(2)]
    sketch_out[0] = tiles[0]
    sketch_out[1] = tiles[1]
    even = jnp.full((8, LANES), core[0], jnp.int32) == 0
    value = jnp.concatenate(tiles, axis=1)
    high = value.astype(bf16)
    middle, low = split(value - high.astype(f32))
    left = jnp.concatenate(
        [part.astype(f32) for part in (high, middle, low, jnp.zeros_like(low))], axis=0
    ).astype(bf16)
    for c in range(4):
        terms = jnp.dot(left, merged_out[:, c * 1024 : (c + 1) * 1024], preferred_element_type=f32)
        total = terms[:8] + (terms[8:16] + terms[16:24])
        for t in range(4):
            first = 2 * t * LANES
            zero = total[:, first : first + LANES]
            one = total[:, first + LANES : first + 2 * LANES]
            keep[4 * c + t, 0] = jnp.where(even, zero, one)
            give[4 * c + t, 0] = jnp.where(even, one, zero)


def third(received, send):
    tiles = [total_of(received, k) for k in range(3)]
    for z in range(8):
        for k in range(3):
            send[z, k] = tiles[k]


def fourth(received, send):
    tiles = [total_of(received, k) for k in range(3)]
    for t in range(16):
        for k in range(3):
            send[t, k] = tiles[k]


def in_order(core, mine, other, first, count):
    even = jnp.full((8, LANES), core[0], jnp.int32) == 0
    tiles = []
    for t in range(16):
        for k in range(first, first + count):
            tiles.append(jnp.where(even, mine[t, k], other[t, k]))
        for k in range(first, first + count):
            tiles.append(jnp.where(even, other[t, k], mine[t, k]))
    return tiles


def partial_factor(core, which, tiles, merged_kv):
    base = lax.rem(core[0] + which, 2) * 256
    term = jnp.zeros((16, LANES), f32)
    for t in range(16):
        high, low = split(jnp.concatenate([tiles[t, 0], tiles[t, 1]], axis=1))
        left = jnp.concatenate([high.astype(f32), low.astype(f32)], axis=0).astype(bf16)
        rows = pl.ds(pl.multiple_of(t * 512 + base, 256), 256)
        term = term + jnp.dot(left, merged_kv[rows, :], preferred_element_type=f32)
    return term[:8] + term[8:]


def fifth_mine(core, mine, merged_kv, term):
    term[...] = partial_factor(core, 0, mine, merged_kv)


def fifth_other(core, other, merged_kv, begun, send):
    term = begun[...] + partial_factor(core, 1, other, merged_kv)
    for d in range(16):
        send[d] = term


def orthonormal_kv(core, mine, other, basis, lower, scale):
    tiles = in_order(core, mine, other, 0, 2)
    steps, inverse = cholesky(gram_columns(tiles))
    for j in range(8):
        lower[j] = steps[j]
    scale[...] = inverse
    for k, tile in enumerate(tiles):
        basis[:, k * LANES : (k + 1) * LANES] = substitute(tile, steps, inverse)


def finish_out(core, mine, other, warm, sketch_out, merged_out, factor, residual, near, done,
               factor_near, warm_near, arrived, sent, factor_sent, warm_arrived):
    wide = done.shape[1] // 4

    def arriving(c):
        part = block(c, wide)
        return pltpu.make_async_copy(merged_out.at[:, part], near.at[:, part], arrived.at[c])

    def leaving(c):
        part = block(c, wide)
        return pltpu.make_async_copy(done.at[:, part], residual.at[:, part], sent.at[c])

    warm_copy = pltpu.make_async_copy(warm, warm_near, warm_arrived)
    warm_copy.start()

    @pl.loop(0, 4)
    def _(c):
        arriving(c).start()

    values = in_order(core, mine, other, 2, 1)
    warm_copy.wait()
    sums = [jnp.zeros((8, LANES), f32)] * 8
    for k, tile in enumerate(values):
        right = warm_near[:, k * LANES : (k + 1) * LANES].astype(bf16).astype(f32)
        for j in range(8):
            sums[j] = sums[j] + right * row(tile, j)
    steps, scale = cholesky(
        [jnp.broadcast_to(jnp.sum(total, axis=1, keepdims=True), (8, LANES)) for total in sums]
    )
    basis = [substitute(sketch_out[k], steps, scale) for k in range(2)]
    left = left_terms(jnp.concatenate(basis, axis=1))
    values = [substitute(tile, steps, scale) * (1.0 / 16.0) for tile in values]
    for k, value in enumerate(values):
        factor_near[:, k * LANES : (k + 1) * LANES] = value
    factor_copy = pltpu.make_async_copy(factor_near, factor, factor_sent)
    factor_copy.start()
    for c in range(4):
        right = right_terms(jnp.concatenate(values[8 * c : 8 * c + 8], axis=1))
        part = block(c, wide)
        approx = jnp.dot(left, right, preferred_element_type=f32)
        arriving(c).wait()
        done[:, part] = (near[:, part].astype(f32) - approx).astype(bf16)
        leaving(c).start()

    @pl.loop(0, 4)
    def _(c):
        leaving(c).wait()

    factor_copy.wait()


def finish_kv(received, lower, scale, basis, merged_kv, factor, residual, done, factor_near, sent,
              factor_sent):
    rows = 1024

    def leaving(c):
        part = block(c, rows)
        return pltpu.make_async_copy(done.at[part], residual.at[part], sent.at[c])

    value = received[0]
    for d in range(1, 16):
        value = value + received[d]
    value = substitute(value, [lower[j] for j in range(8)], scale[...]) * (1.0 / 16.0)
    factor_near[...] = value
    factor_copy = pltpu.make_async_copy(factor_near, factor, factor_sent)
    factor_copy.start()
    right = right_terms(value)
    for c in range(8):
        part = block(c, rows)
        left = left_terms(basis[:, part])
        approx = jnp.dot(left, right, preferred_element_type=f32)
        done[part, :] = (merged_kv[part, :].astype(f32) - approx).astype(bf16)
        leaving(c).start()

    @pl.loop(0, 8)
    def _(c):
        leaving(c).wait()

    factor_copy.wait()


def exchange(value, axis, groups=None):
    return lax.all_to_all(value, axis, 0, 0, axis_index_groups=groups)


def call(kernel, outs, ins, args, scratch=(), seconds=1.0, aliases=None):
    return pl.pallas_call(
        kernel,
        out_shape=outs,
        in_specs=ins,
        out_specs=jax.tree.map(
            lambda out: far if isinstance(out, pl.MemoryRef) and out.memory_space == pltpu.HBM else whole,
            outs,
            is_leaf=lambda out: not isinstance(out, tuple),
        ),
        scratch_shapes=list(scratch),
        input_output_aliases=aliases or {},
        compiler_params=limit,
        cost_estimate=pl.CostEstimate(
            flops=0, bytes_accessed=int(seconds * 2_000_000), transcendentals=0
        ),
        name=kernel.__name__,
    )(*args)


far = pl.BlockSpec(memory_space=pltpu.HBM)
scalar = pl.BlockSpec(memory_space=pltpu.SMEM)


def per_device(grad_kv, error_kv, grad_out, error_out, warm_kv, warm_out):
    grad_kv, error_kv, grad_out, error_out = (
        distant(value[0]) for value in (grad_kv, error_kv, grad_out, error_out)
    )
    kv_shape, out_shape = grad_kv.shape, grad_out.shape
    columns = [[2 * z + c for z in range(8)] for c in range(2)]
    swap = [(d, d ^ 1) for d in range(16)]
    core = (lax.axis_index("dp") % 2).astype(jnp.int32).reshape(1)

    def tiles(*lead):
        return pltpu.VMEM((*lead, 8, LANES), f32)

    merged_out, send = call(
        first_out,
        (pltpu.VMEM(out_shape, bf16), tiles(16, 2)),
        [far] * 3,
        (grad_out, error_out, distant(warm_out.T)),
        [
            pltpu.VMEM((8, out_shape[1]), f32),
            pltpu.VMEM(out_shape, bf16),
            pltpu.VMEM(out_shape, bf16),
            pltpu.SemaphoreType.DMA((2, OUT_CHUNKS)),
            pltpu.SemaphoreType.DMA,
        ],
        2.6,
    )
    received = exchange(send, "dp")
    merged_kv, stored, keep_kv, give_kv = call(
        first_kv,
        (pltpu.HBM(kv_shape, bf16), pltpu.HBM(out_shape, bf16), tiles(16, 2), tiles(16, 2)),
        [scalar] + [far] * 3 + [whole],
        (core, grad_kv, error_kv, distant(warm_kv.T), resident(merged_out)),
        [
            pltpu.VMEM((8, kv_shape[1]), f32),
            pltpu.VMEM(kv_shape, bf16),
            pltpu.VMEM(kv_shape, bf16),
            pltpu.VMEM(kv_shape, bf16),
            pltpu.SemaphoreType.DMA((2, KV_CHUNKS)),
            pltpu.SemaphoreType.DMA((KV_CHUNKS,)),
            pltpu.SemaphoreType.DMA,
            pltpu.SemaphoreType.DMA,
        ],
        2.6,
    )
    keep_out, give_out, sketch_out, merged_kv = call(
        second,
        (tiles(16, 1), tiles(16, 1), tiles(2), pltpu.HBM(kv_shape, bf16)),
        [scalar] + [whole] * 2 + [far],
        (core, resident(received), resident(merged_out), distant(merged_kv)),
        seconds=0.4,
        aliases={3: 3},
    )
    kv = keep_kv + lax.ppermute(give_kv, "dp", swap)
    out = keep_out + lax.ppermute(give_out, "dp", swap)
    received = exchange(jnp.concatenate([kv, out], axis=1), "tensor")
    send = call(third, tiles(8, 3), [whole], (resident(received),), seconds=0.1)
    received = exchange(send, "dp", columns)
    send = call(fourth, tiles(16, 3), [whole], (resident(received),), seconds=0.1)
    mine = exchange(send, "tensor")
    other = lax.ppermute(mine, "dp", swap)
    begun = call(
        fifth_mine,
        tiles(),
        [scalar] + [whole] * 2,
        (core, resident(mine), resident(merged_kv)),
        seconds=0.5,
    )
    send = call(
        fifth_other,
        tiles(16),
        [scalar] + [whole] * 3,
        (core, resident(other), resident(merged_kv), resident(begun)),
        seconds=0.5,
    )
    received = exchange(send, "dp")
    basis, lower, scale = call(
        orthonormal_kv,
        (pltpu.VMEM((8, kv_shape[0]), f32), tiles(8), tiles()),
        [scalar] + [whole] * 2,
        (core, resident(mine), resident(other)),
    )
    factor_out, residual_out = call(
        finish_out,
        (pltpu.HBM((8, out_shape[1]), f32), pltpu.HBM(out_shape, bf16)),
        [scalar] + [whole] * 2 + [far, whole, far],
        (
            core,
            resident(mine),
            resident(other),
            distant(warm_out.T),
            resident(sketch_out),
            distant(stored),
        ),
        [
            pltpu.VMEM(out_shape, bf16),
            pltpu.VMEM(out_shape, bf16),
            pltpu.VMEM((8, out_shape[1]), f32),
            pltpu.VMEM((8, out_shape[1]), f32),
            pltpu.SemaphoreType.DMA((4,)),
            pltpu.SemaphoreType.DMA((4,)),
            pltpu.SemaphoreType.DMA,
            pltpu.SemaphoreType.DMA,
        ],
        2.5,
    )
    factor_kv, residual_kv = call(
        finish_kv,
        (pltpu.HBM((8, kv_shape[1]), f32), pltpu.HBM(kv_shape, bf16)),
        [whole] * 5,
        tuple(resident(value) for value in (received, lower, scale, basis, merged_kv)),
        [
            pltpu.VMEM(kv_shape, bf16),
            pltpu.VMEM((8, kv_shape[1]), f32),
            pltpu.SemaphoreType.DMA((8,)),
            pltpu.SemaphoreType.DMA,
        ],
        2.5,
    )
    return factor_kv.T, factor_out.T, residual_kv[None], residual_out[None]


def solution(mesh):
    placed = (
        P("dp", None, "tensor"),
        P("dp", None, "tensor"),
        P("dp", "tensor", None),
        P("dp", "tensor", None),
        P("tensor", None),
        P(),
    )
    return jax.shard_map(
        per_device,
        mesh=mesh,
        in_specs=placed,
        out_specs=(P("tensor", None), P(), P("dp", None, "tensor"), P("dp", "tensor", None)),
        check_vma=False,
    )
```

time: 931 us -> 78.5 us (0.08)
  blocking collectives: 502 us -> 34.1 us
  waiting for transfers between devices: 349 us -> 10.3 us
  matrix products: 33.4 us -> 0 us
  between operations: 25.4 us -> 0.73 us
  other arithmetic: 17.9 us -> 0.04 us
  starting transfers between devices: 0.04 us -> 17.8 us
  Pallas kernels: 0 us -> 15.1 us
    psum x17 -> x0, blocking collectives: 502 us -> none  [the longest x8 249 us: length_total(): return lax.psum(values, 'tensor')]
    psum x1 -> x0, waiting for transfers between devices: 349 us -> none  [per_device(): sketch_kv = lax.psum(partial_kv, ('dp', 'tensor'))]
    all_to_all x0 -> x3, blocking collectives: none -> 34.1 us  [exchange(): return lax.all_to_all(value, axis, 0, 0, axis_index_groups=groups)]
    dot_general x30 -> x0, matrix products: 33.4 us -> none  [the longest x1 9.26 us: per_device(): jnp.dot(basis_kv, factor_kv.T, precision=highest, preferred_element_type=...]
    pallas_call x0 -> x10, Pallas kernels: none -> 15.1 us  [call(): pl.pallas_call(kernel, out_shape=outs, in_specs=ins, out_specs=jax.tree.m...]
    all_to_all x0 -> x2, starting transfers between devices: none -> 13.6 us  [exchange(): return lax.all_to_all(value, axis, 0, 0, axis_index_groups=groups)]
    reduce_sum x16 -> x0, other arithmetic: 12.1 us -> none  [orthonormal(): squares = tuple((jnp.sum(vector * vector) for vector in vectors))]
  transfers between devices with their start and end apart: 1 -> 5, of which waited for: 1 -> 4; matrix products, arithmetic and copies ran while one was open for 0% -> 0% of each run, Pallas kernels for 0% -> 12%
where the time goes in v2:
time: 78.5 us; the launch traced here: 78.1 us
  blocking collectives  34.1 us (43%)
  starting transfers between devices  17.8 us (23%)
  Pallas kernels  15.1 us (19%)
  waiting for transfers between devices  10.3 us (13%)
    all_to_all x3, blocking collectives, exchange(): return lax.all_to_all(value, axis, 0, 0, axis_index_groups=groups)  34.1 us
    pallas_call x10, Pallas kernels, call(): pl.pallas_call(kernel, out_shape=outs, in_specs=ins, out_specs=jax.tree.m...  15.1 us
    all_to_all x2, starting transfers between devices, exchange(): return lax.all_to_all(value, axis, 0, 0, axis_index_groups=groups)  13.6 us
    all_to_all x2, waiting for transfers between devices, exchange(): return lax.all_to_all(value, axis, 0, 0, axis_index_groups=groups)  8.3 us
    ppermute x1, starting transfers between devices, per_device(): other = lax.ppermute(mine, 'dp', swap)  3.85 us
  transfers between devices with their start and end apart: 5, of which 4 were waited for; matrix products, arithmetic and copies ran while one was open for 0% of the time, Pallas kernels for 12%

profile of v2, /device:TPU:1, one launch (start us, length us, event | category | flops | bytes accessed | tf_op | source)
XLA Modules:
  0.0 78.1 jit_solution(5130842312931447209)
XLA Ops:
  0.6 3.2 %first_out.1 = (bf16[256,4096]{1,0:T(8,128)(2,1)S(1)}, f32[16,2,8,128]{3,2,1,0:T(8,128)}) custom-call(bf16[256,4096]{1,0:T(8,128)(2,1)} %bitcast.11, bf16[256,4096]{1,0:T(8,128)(2,1)} %bitcast.12, f32[8,4096]{1,0:T(8,128)} %bitcast.15), custom_call_target="tpu_custom_call" | custom-call | bytes 5200000 | tf_op jit(solution)/shard_map/first_out/pallas_call | solution.py:356
  3.9 10.0 %all-to-all-start = ((f32[16,2,8,128]{3,2,1,0:T(8,128)}), f32[16,2,8,128]{3,2,1,0:T(8,128)S(1)}, u32[]{:S(2)}, u32[]{:S(2)}) async-start(f32[16,2,8,128]{3,2,1,0:T(8,128)} %get-tuple-element.24), calls=%async_computation | async-start | bytes 262144 | tf_op jit(solution)/shard_map/all_to_all | solution.py:352
  13.9 4.3 %first_kv.1 = (bf16[8192,128]{1,0:T(8,128)(2,1)}, bf16[256,4096]{1,0:T(8,128)(2,1)}, f32[16,2,8,128]{3,2,1,0:T(8,128)S(1)}, f32[16,2,8,128]{3,2,1,0:T(8,128)S(1)}) custom-call(s32[1]{0:T(128)} %bitcast.core, bf16[8192,128]{1,0:T(8,128)(2,1)} %bitcast.13, bf16[8192,128]{1,0:T(8,128)(2,1)} %bitcast.14, f32[8,128]{1,0:T(8,128)} %bitcast.17, ...), custom_call_target="tpu_custom_call" | custom-call | bytes 5200000 | tf_op jit(solution)/shard_map/first_kv/pallas_call | solution.py:356
  18.2 0.2 collective-permute-start
  18.4 4.6 %all-to-all-done.received = f32[16,2,8,128]{3,2,1,0:T(8,128)S(1)} async-done(((f32[16,2,8,128]{3,2,1,0:T(8,128)}), f32[16,2,8,128]{3,2,1,0:T(8,128)S(1)}, u32[]{:S(2)}, u32[]{:S(2)}) %all-to-all-start) | async-done | bytes 131104 | tf_op jit(solution)/shard_map/all_to_all | solution.py:352
  23.0 0.4 second.1
  23.5 0.0 copy-start
  23.5 0.1 collective-permute-start.1
  23.6 0.0 collective-permute-done
  23.6 1.2 %collective-permute-done.1 = f32[16,1,8,128]{3,2,1,0:T(8,128)S(1)} collective-permute-done((f32[16,1,8,128]{3,2,1,0:T(8,128)S(1)}, f32[16,1,8,128]{3,2,1,0:T(8,128)S(1)}, u32[]{:S(2)}, u32[]{:S(2)}) %collective-permute-start.1) | collective-permute-done | bytes 65568 | tf_op jit(solution)/shard_map/ppermute | solution.py:432
  24.9 13.6 %all_to_all.25.received = f32[16,3,8,128]{3,2,1,0:T(8,128)S(1)} all-to-all(f32[16,3,8,128]{3,2,1,0:T(8,128)S(1)} %pad_maximum_fusion), channel_id=1, replica_groups=mesh['dp'=16,'tensor'=16] {'tensor'}, dimensions={0} | all-to-all | bytes 393216 | tf_op jit(solution)/shard_map/all_to_all | solution.py:352
  38.5 10.0 %all_to_all.26.received = f32[8,3,8,128]{3,2,1,0:T(8,128)S(1)} all-to-all(f32[8,3,8,128]{3,2,1,0:T(8,128)S(1)} %third.1), channel_id=1, replica_groups={{0,32,64,96,128,160,192,224},{16,48,80,112,144,176,208,240},{1,33,65,97..., dimensions={0} | all-to-all | bytes 196608 | tf_op jit(solution)/shard_map/all_to_all | solution.py:352
  48.5 10.5 %all_to_all.27.mine = f32[16,3,8,128]{3,2,1,0:T(8,128)S(1)} all-to-all(f32[16,3,8,128]{3,2,1,0:T(8,128)S(1)} %fourth.1), channel_id=1, replica_groups=mesh['dp'=16,'tensor'=16] {'tensor'}, dimensions={0} | all-to-all | bytes 393216 | tf_op jit(solution)/shard_map/all_to_all | solution.py:352
  59.0 3.8 %collective-permute-start.2 = (f32[16,3,8,128]{3,2,1,0:T(8,128)S(1)}, f32[16,3,8,128]{3,2,1,0:T(8,128)S(1)}, u32[]{:S(2)}, u32[]{:S(2)}) collective-permute-start(f32[16,3,8,128]{3,2,1,0:T(8,128)S(1)} %all_to_all.27.mine), channel_id=1, source_target_pairs={{0,16},{16,0},{32,48},{48,32},{64,80},{80,64},{96,112},{112,96},{1... | collective-permute-start | bytes 589832 | tf_op jit(solution)/shard_map/ppermute | solution.py:438
  62.9 0.0 copy-done
  62.9 0.2 fifth_mine.1.begun
  63.1 0.8 %collective-permute-done.2.other = f32[16,3,8,128]{3,2,1,0:T(8,128)S(1)} collective-permute-done((f32[16,3,8,128]{3,2,1,0:T(8,128)S(1)}, f32[16,3,8,128]{3,2,1,0:T(8,128)S(1)}, u32[]{:S(2)}, u32[]{:S(2)}) %collective-permute-start.2) | collective-permute-done | bytes 196640 | tf_op jit(solution)/shard_map/ppermute | solution.py:438
  63.9 0.9 %fifth_other.1 = f32[16,8,128]{2,1,0:T(8,128)} custom-call(s32[1]{0:T(128)} %bitcast.core, f32[16,3,8,128]{3,2,1,0:T(8,128)S(1)} %collective-permute-done.2.other, bf16[8192,128]{1,0:T(8,128)(2,1)S(1)} %copy-done, f32[8,128]{1,0:T(8,128)S(1)} %fifth_mine.1.begun), custom_call_target="tpu_custom_call" | custom-call | bytes 1000000 | tf_op jit(solution)/shard_map/fifth_other/pallas_call | solution.py:356
  64.8 3.6 %all-to-all-start.4 = ((f32[16,8,128]{2,1,0:T(8,128)}), f32[16,8,128]{2,1,0:T(8,128)S(1)}, u32[]{:S(2)}, u32[]{:S(2)}) async-start(f32[16,8,128]{2,1,0:T(8,128)} %fifth_other.1), calls=%async_computation.4 | async-start | bytes 131072 | tf_op jit(solution)/shard_map/all_to_all | solution.py:352
  68.5 0.5 orthonormal_kv.1
  68.9 3.7 %finish_out.1 = (f32[8,4096]{1,0:T(8,128)}, bf16[256,4096]{1,0:T(8,128)(2,1)}) custom-call(s32[1]{0:T(128)} %bitcast.core, f32[16,3,8,128]{3,2,1,0:T(8,128)S(1)} %all_to_all.27.mine, f32[16,3,8,128]{3,2,1,0:T(8,128)S(1)} %collective-permute-done.2.other, f32[8,4096]{1,0:T(8,128)} %bitcast.16, f32[2,8,128]{2,1,0:T(8,128)S(1)} %get-tuple-element.33.sketch_out, ...), custom_call_target="tpu_custom_call" | custom-call | bytes 5000000 | tf_op jit(solution)/shard_map/finish_out/pallas_call | solution.py:356
  72.6 3.7 %all-to-all-done.4.received = f32[16,8,128]{2,1,0:T(8,128)S(1)} async-done(((f32[16,8,128]{2,1,0:T(8,128)}), f32[16,8,128]{2,1,0:T(8,128)S(1)}, u32[]{:S(2)}, u32[]{:S(2)}) %all-to-all-start.4) | async-done | bytes 65568 | tf_op jit(solution)/shard_map/all_to_all | solution.py:352
  76.3 1.8 %finish_kv.1 = (f32[8,128]{1,0:T(8,128)}, bf16[8192,128]{1,0:T(8,128)(2,1)}) custom-call(f32[16,8,128]{2,1,0:T(8,128)S(1)} %all-to-all-done.4.received, f32[8,8,128]{2,1,0:T(8,128)S(1)} %get-tuple-element.29.lower, f32[8,128]{1,0:T(8,128)S(1)} %get-tuple-element.30.scale, f32[8,8192]{1,0:T(8,128)S(1)} %get-tuple-element.31.basis, bf16[8192,128]{1,0:T(8,128)(2,1)S(1)} %copy-done), custom_call_target="tpu_custom_call" | custom-call | bytes 5000000 | tf_op jit(solution)/shard_map/finish_kv/pallas_call | solution.py:356
  (5 shorter events, 0.1 us)
Async XLA Ops:
  3.9 19.2 %all-to-all-start = ((f32[16,2,8,128]{3,2,1,0:T(8,128)}), f32[16,2,8,128]{3,2,1,0:T(8,128)S(1)}, u32[]{:S(2)}, u32[]{:S(2)}) async-start(f32[16,2,8,128]{3,2,1,0:T(8,128)} %get-tuple-element.24), calls=%async_computation | async-start | bytes 262144 | tf_op jit(solution)/shard_map/all_to_all | solution.py:352
  18.2 5.4 %collective-permute-start = (f32[16,2,8,128]{3,2,1,0:T(8,128)S(1)}, f32[16,2,8,128]{3,2,1,0:T(8,128)S(1)}, u32[]{:S(2)}, u32[]{:S(2)}) collective-permute-start(f32[16,2,8,128]{3,2,1,0:T(8,128)S(1)} %get-tuple-element.23), channel_id=1, source_target_pairs={{0,16},{16,0},{32,48},{48,32},{64,80},{80,64},{96,112},{112,96},{1... | collective-permute-start | bytes 393224 | tf_op jit(solution)/shard_map/ppermute | solution.py:431
  23.5 39.4 %copy-start = (bf16[8192,128]{1,0:T(8,128)(2,1)S(1)}, bf16[8192,128]{1,0:T(8,128)(2,1)}, u32[]{:S(2)}) copy-start(bf16[8192,128]{1,0:T(8,128)(2,1)} %get-tuple-element.28.merged_kv) | copy-start | bytes 6291460
  23.5 1.3 %collective-permute-start.1 = (f32[16,1,8,128]{3,2,1,0:T(8,128)S(1)}, f32[16,1,8,128]{3,2,1,0:T(8,128)S(1)}, u32[]{:S(2)}, u32[]{:S(2)}) collective-permute-start(f32[16,1,8,128]{3,2,1,0:T(8,128)S(1)} %get-tuple-element.27), channel_id=1, source_target_pairs={{0,16},{16,0},{32,48},{48,32},{64,80},{80,64},{96,112},{112,96},{1... | collective-permute-start | bytes 196616 | tf_op jit(solution)/shard_map/ppermute | solution.py:432
  59.0 4.9 %collective-permute-start.2 = (f32[16,3,8,128]{3,2,1,0:T(8,128)S(1)}, f32[16,3,8,128]{3,2,1,0:T(8,128)S(1)}, u32[]{:S(2)}, u32[]{:S(2)}) collective-permute-start(f32[16,3,8,128]{3,2,1,0:T(8,128)S(1)} %all_to_all.27.mine), channel_id=1, source_target_pairs={{0,16},{16,0},{32,48},{48,32},{64,80},{80,64},{96,112},{112,96},{1... | collective-permute-start | bytes 589832 | tf_op jit(solution)/shard_map/ppermute | solution.py:438
  64.8 11.5 %all-to-all-start.4 = ((f32[16,8,128]{2,1,0:T(8,128)}), f32[16,8,128]{2,1,0:T(8,128)S(1)}, u32[]{:S(2)}, u32[]{:S(2)}) async-start(f32[16,8,128]{2,1,0:T(8,128)} %fifth_other.1), calls=%async_computation.4 | async-start | bytes 131072 | tf_op jit(solution)/shard_map/all_to_all | solution.py:352

commit v3 on v2

--- a/solution.py
+++ b/solution.py
@@ -188,27 +188,33 @@
     return value
 
 
-def second(core, received, merged_out, merged_kv, keep, give, sketch_out, same_kv):
-    del merged_kv, same_kv
+def half_factor(left, merged_out, half, target):
+    wide = merged_out.shape[1] // 4
+    for c in range(2):
+        part = pl.ds(pl.multiple_of((2 * half + c) * wide, wide), wide)
+        terms = jnp.dot(left, merged_out[:, part], preferred_element_type=f32)
+        total = terms[:8] + (terms[8:16] + terms[16:24])
+        for t in range(8):
+            target[8 * c + t, 0] = total[:, t * LANES : (t + 1) * LANES]
+
+
+def second_give(core, received, merged_out, give, sketch_out, terms):
     tiles = [total_of(received, k) for k in range(2)]
     sketch_out[0] = tiles[0]
     sketch_out[1] = tiles[1]
-    even = jnp.full((8, LANES), core[0], jnp.int32) == 0
     value = jnp.concatenate(tiles, axis=1)
     high = value.astype(bf16)
     middle, low = split(value - high.astype(f32))
     left = jnp.concatenate(
         [part.astype(f32) for part in (high, middle, low, jnp.zeros_like(low))], axis=0
     ).astype(bf16)
-    for c in range(4):
-        terms = jnp.dot(left, merged_out[:, c * 1024 : (c + 1) * 1024], preferred_element_type=f32)
-        total = terms[:8] + (terms[8:16] + terms[16:24])
-        for t in range(4):
-            first = 2 * t * LANES
-            zero = total[:, first : first + LANES]
-            one = total[:, first + LANES : first + 2 * LANES]
-            keep[4 * c + t, 0] = jnp.where(even, zero, one)
-            give[4 * c + t, 0] = jnp.where(even, one, zero)
+    terms[...] = left
+    half_factor(left, merged_out, 1 - core[0], give)
+
+
+def second_keep(core, terms, merged_out, merged_kv, keep, same_kv):
+    del merged_kv, same_kv
+    half_factor(terms[...], merged_out, core[0], keep)
 
 
 def third(received, send):
@@ -225,13 +231,13 @@
             send[t, k] = tiles[k]
 
 
-def in_order(core, mine, other, first, count):
+def in_order(core, mine, other):
     even = jnp.full((8, LANES), core[0], jnp.int32) == 0
     tiles = []
     for t in range(16):
-        for k in range(first, first + count):
+        for k in range(2):
             tiles.append(jnp.where(even, mine[t, k], other[t, k]))
-        for k in range(first, first + count):
+        for k in range(2):
             tiles.append(jnp.where(even, other[t, k], mine[t, k]))
     return tiles
 
@@ -258,7 +264,7 @@
 
 
 def orthonormal_kv(core, mine, other, basis, lower, scale):
-    tiles = in_order(core, mine, other, 0, 2)
+    tiles = in_order(core, mine, other)
     steps, inverse = cholesky(gram_columns(tiles))
     for j in range(8):
         lower[j] = steps[j]
@@ -286,7 +292,9 @@
     def _(c):
         arriving(c).start()
 
-    values = in_order(core, mine, other, 2, 1)
+    even = jnp.full((8, LANES), core[0], jnp.int32) == 0
+    values = [jnp.where(even, mine[t, 2], other[t, 2]) for t in range(16)]
+    values += [jnp.where(even, other[t, 2], mine[t, 2]) for t in range(16)]
     warm_copy.wait()
     sums = [jnp.zeros((8, LANES), f32)] * 8
     for k, tile in enumerate(values):
@@ -381,8 +389,15 @@
         distant(value[0]) for value in (grad_kv, error_kv, grad_out, error_out)
     )
     kv_shape, out_shape = grad_kv.shape, grad_out.shape
-    columns = [[2 * z + c for z in range(8)] for c in range(2)]
+    columns = [[2 * z for z in range(8)], [2 * z + 1 for z in reversed(range(8))]]
+    replicas = [[2 * z for z in range(8)] + [2 * z + 1 for z in range(8)]]
     swap = [(d, d ^ 1) for d in range(16)]
+    other_way = [15 - t for t in range(16)]
+    planes = [
+        [(2 * z + c) * 16 + (t if c == 0 else other_way[t]) for t in range(16)]
+        for z in range(8)
+        for c in range(2)
+    ]
     core = (lax.axis_index("dp") % 2).astype(jnp.int32).reshape(1)
 
     def tiles(*lead):
@@ -402,7 +417,7 @@
         ],
         2.6,
     )
-    received = exchange(send, "dp")
+    received = exchange(send, "dp", replicas)
     merged_kv, stored, keep_kv, give_kv = call(
         first_kv,
         (pltpu.HBM(kv_shape, bf16), pltpu.HBM(out_shape, bf16), tiles(16, 2), tiles(16, 2)),
@@ -420,21 +435,28 @@
         ],
         2.6,
     )
-    keep_out, give_out, sketch_out, merged_kv = call(
-        second,
-        (tiles(16, 1), tiles(16, 1), tiles(2), pltpu.HBM(kv_shape, bf16)),
+    give_out, sketch_out, terms = call(
+        second_give,
+        (tiles(16, 1), tiles(2), pltpu.VMEM((32, out_shape[0]), bf16)),
+        [scalar] + [whole] * 2,
+        (core, resident(received), resident(merged_out)),
+        seconds=0.3,
+    )
+    keep_out, merged_kv = call(
+        second_keep,
+        (tiles(16, 1), pltpu.HBM(kv_shape, bf16)),
         [scalar] + [whole] * 2 + [far],
-        (core, resident(received), resident(merged_out), distant(merged_kv)),
-        seconds=0.4,
-        aliases={3: 3},
+        (core, resident(terms), resident(merged_out), distant(merged_kv)),
+        seconds=0.2,
+        aliases={3: 1},
     )
     kv = keep_kv + lax.ppermute(give_kv, "dp", swap)
     out = keep_out + lax.ppermute(give_out, "dp", swap)
-    received = exchange(jnp.concatenate([kv, out], axis=1), "tensor")
+    received = exchange(jnp.concatenate([kv, out], axis=1), ("dp", "tensor"), planes)
     send = call(third, tiles(8, 3), [whole], (resident(received),), seconds=0.1)
     received = exchange(send, "dp", columns)
     send = call(fourth, tiles(16, 3), [whole], (resident(received),), seconds=0.1)
-    mine = exchange(send, "tensor")
+    mine = exchange(send, ("dp", "tensor"), planes)
     other = lax.ppermute(mine, "dp", swap)
     begun = call(
         fifth_mine,
@@ -450,7 +472,7 @@
         (core, resident(other), resident(merged_kv), resident(begun)),
         seconds=0.5,
     )
-    received = exchange(send, "dp")
+    received = exchange(send, "dp", replicas)
     basis, lower, scale = call(
         orthonormal_kv,
         (pltpu.VMEM((8, kv_shape[0]), f32), tiles(8), tiles()),

time: 78.5 us -> 77.5 us (0.987)
  starting transfers between devices: 17.8 us -> 21.9 us
  waiting for transfers between devices: 10.3 us -> 7.19 us
  blocking collectives: 34.1 us -> 32.2 us
    ppermute x1, starting transfers between devices: 3.85 us -> 6.6 us  [per_device(): other = lax.ppermute(mine, 'dp', swap)]
    all_to_all x2, waiting for transfers between devices: 8.3 us -> 5.76 us  [exchange(): return lax.all_to_all(value, axis, 0, 0, axis_index_groups=groups)]
    all_to_all x3, blocking collectives: 34.1 us -> 32.2 us  [exchange(): return lax.all_to_all(value, axis, 0, 0, axis_index_groups=groups)]
    ppermute x1, starting transfers between devices: 0.09 us -> 1.35 us  [per_device(): out = keep_out + lax.ppermute(give_out, 'dp', swap)]
    pallas_call x10 -> x11, Pallas kernels: 15.1 us -> 15.2 us  [call(): pl.pallas_call(kernel, out_shape=outs, in_specs=ins, out_specs=jax.tree.m...]
where the time goes in v3:
time: 77.5 us; the launch traced here: 77.2 us
  blocking collectives  32.2 us (42%)
  starting transfers between devices  21.9 us (28%)
  Pallas kernels  15.2 us (20%)
  waiting for transfers between devices  7.19 us (9%)
    all_to_all x3, blocking collectives, exchange(): return lax.all_to_all(value, axis, 0, 0, axis_index_groups=groups)  32.2 us
    pallas_call x11, Pallas kernels, call(): pl.pallas_call(kernel, out_shape=outs, in_specs=ins, out_specs=jax.tree.m...  15.2 us
    all_to_all x2, starting transfers between devices, exchange(): return lax.all_to_all(value, axis, 0, 0, axis_index_groups=groups)  13.7 us
    ppermute x1, starting transfers between devices, per_device(): other = lax.ppermute(mine, 'dp', swap)  6.6 us
    all_to_all x2, waiting for transfers between devices, exchange(): return lax.all_to_all(value, axis, 0, 0, axis_index_groups=groups)  5.76 us
  transfers between devices with their start and end apart: 5, of which 4 were waited for; matrix products, arithmetic and copies ran while one was open for 0% of the time, Pallas kernels for 12%

profile of v3, /device:TPU:1, one launch (start us, length us, event | category | flops | bytes accessed | tf_op | source)
XLA Modules:
  0.0 77.2 jit_solution(4441844821917456273)
XLA Ops:
  0.6 3.2 %first_out.1 = (bf16[256,4096]{1,0:T(8,128)(2,1)S(1)}, f32[16,2,8,128]{3,2,1,0:T(8,128)}) custom-call(bf16[256,4096]{1,0:T(8,128)(2,1)} %bitcast.11, bf16[256,4096]{1,0:T(8,128)(2,1)} %bitcast.12, f32[8,4096]{1,0:T(8,128)} %bitcast.15), custom_call_target="tpu_custom_call" | custom-call | bytes 5200000 | tf_op jit(solution)/shard_map/first_out/pallas_call | solution.py:364
  3.9 10.0 %all-to-all-start = ((f32[16,2,8,128]{3,2,1,0:T(8,128)}), f32[16,2,8,128]{3,2,1,0:T(8,128)S(1)}, u32[]{:S(2)}, u32[]{:S(2)}) async-start(f32[16,2,8,128]{3,2,1,0:T(8,128)} %get-tuple-element.25), calls=%async_computation | async-start | bytes 262144 | tf_op jit(solution)/shard_map/all_to_all | solution.py:360
  13.9 4.3 %first_kv.1 = (bf16[8192,128]{1,0:T(8,128)(2,1)}, bf16[256,4096]{1,0:T(8,128)(2,1)}, f32[16,2,8,128]{3,2,1,0:T(8,128)S(1)}, f32[16,2,8,128]{3,2,1,0:T(8,128)S(1)}) custom-call(s32[1]{0:T(128)} %bitcast.core, bf16[8192,128]{1,0:T(8,128)(2,1)} %bitcast.13, bf16[8192,128]{1,0:T(8,128)(2,1)} %bitcast.14, f32[8,128]{1,0:T(8,128)} %bitcast.17, ...), custom_call_target="tpu_custom_call" | custom-call | bytes 5200000 | tf_op jit(solution)/shard_map/first_kv/pallas_call | solution.py:364
  18.2 0.2 collective-permute-start
  18.4 2.8 %all-to-all-done.received = f32[16,2,8,128]{3,2,1,0:T(8,128)S(1)} async-done(((f32[16,2,8,128]{3,2,1,0:T(8,128)}), f32[16,2,8,128]{3,2,1,0:T(8,128)S(1)}, u32[]{:S(2)}, u32[]{:S(2)}) %all-to-all-start) | async-done | bytes 131104 | tf_op jit(solution)/shard_map/all_to_all | solution.py:360
  21.2 0.3 second_give.1
  21.4 1.4 %collective-permute-start.1 = (f32[16,1,8,128]{3,2,1,0:T(8,128)S(1)}, f32[16,1,8,128]{3,2,1,0:T(8,128)S(1)}, u32[]{:S(2)}, u32[]{:S(2)}) collective-permute-start(f32[16,1,8,128]{3,2,1,0:T(8,128)S(1)} %get-tuple-element.29), channel_id=1, source_target_pairs={{0,16},{16,0},{32,48},{48,32},{64,80},{80,64},{96,112},{112,96},{1... | collective-permute-start | bytes 196616 | tf_op jit(solution)/shard_map/ppermute | solution.py:454
  22.8 0.0 collective-permute-done
  22.8 0.3 second_keep.1
  23.1 0.0 copy-start
  23.1 0.6 collective-permute-done.1
  23.7 11.4 %all_to_all.25.received = f32[16,3,8,128]{3,2,1,0:T(8,128)S(1)} all-to-all(f32[16,3,8,128]{3,2,1,0:T(8,128)S(1)} %pad_maximum_fusion), channel_id=1, replica_groups={{0,1,2,3,4,5,6,7,8,9,10,11,12,13,14,15},{31,30,29,28,27,26,25,24,23,22,..., dimensions={0} | all-to-all | bytes 393216 | tf_op jit(solution)/shard_map/all_to_all | solution.py:360
  35.2 9.8 %all_to_all.26.received = f32[8,3,8,128]{3,2,1,0:T(8,128)S(1)} all-to-all(f32[8,3,8,128]{3,2,1,0:T(8,128)S(1)} %third.1), channel_id=1, replica_groups={{0,32,64,96,128,160,192,224},{240,208,176,144,112,80,48,16},{1,33,65,97..., dimensions={0} | all-to-all | bytes 196608 | tf_op jit(solution)/shard_map/all_to_all | solution.py:360
  45.0 10.9 %all_to_all.27.mine = f32[16,3,8,128]{3,2,1,0:T(8,128)S(1)} all-to-all(f32[16,3,8,128]{3,2,1,0:T(8,128)S(1)} %fourth.1), channel_id=1, replica_groups={{0,1,2,3,4,5,6,7,8,9,10,11,12,13,14,15},{31,30,29,28,27,26,25,24,23,22,..., dimensions={0} | all-to-all | bytes 393216 | tf_op jit(solution)/shard_map/all_to_all | solution.py:360
  55.9 6.6 %collective-permute-start.2 = (f32[16,3,8,128]{3,2,1,0:T(8,128)S(1)}, f32[16,3,8,128]{3,2,1,0:T(8,128)S(1)}, u32[]{:S(2)}, u32[]{:S(2)}) collective-permute-start(f32[16,3,8,128]{3,2,1,0:T(8,128)S(1)} %all_to_all.27.mine), channel_id=1, source_target_pairs={{0,16},{16,0},{32,48},{48,32},{64,80},{80,64},{96,112},{112,96},{1... | collective-permute-start | bytes 589832 | tf_op jit(solution)/shard_map/ppermute | solution.py:460
  62.5 0.0 copy-done
  62.5 0.2 fifth_mine.1.begun
  62.8 0.8 %collective-permute-done.2.other = f32[16,3,8,128]{3,2,1,0:T(8,128)S(1)} collective-permute-done((f32[16,3,8,128]{3,2,1,0:T(8,128)S(1)}, f32[16,3,8,128]{3,2,1,0:T(8,128)S(1)}, u32[]{:S(2)}, u32[]{:S(2)}) %collective-permute-start.2) | collective-permute-done | bytes 196640 | tf_op jit(solution)/shard_map/ppermute | solution.py:460
  63.6 0.9 %fifth_other.1 = f32[16,8,128]{2,1,0:T(8,128)} custom-call(s32[1]{0:T(128)} %bitcast.core, f32[16,3,8,128]{3,2,1,0:T(8,128)S(1)} %collective-permute-done.2.other, bf16[8192,128]{1,0:T(8,128)(2,1)S(1)} %copy-done, f32[8,128]{1,0:T(8,128)S(1)} %fifth_mine.1.begun), custom_call_target="tpu_custom_call" | custom-call | bytes 1000000 | tf_op jit(solution)/shard_map/fifth_other/pallas_call | solution.py:364
  64.5 3.7 %all-to-all-start.4 = ((f32[16,8,128]{2,1,0:T(8,128)}), f32[16,8,128]{2,1,0:T(8,128)S(1)}, u32[]{:S(2)}, u32[]{:S(2)}) async-start(f32[16,8,128]{2,1,0:T(8,128)} %fifth_other.1), calls=%async_computation.4 | async-start | bytes 131072 | tf_op jit(solution)/shard_map/all_to_all | solution.py:360
  68.2 0.5 orthonormal_kv.1
  68.7 3.7 %finish_out.1 = (f32[8,4096]{1,0:T(8,128)}, bf16[256,4096]{1,0:T(8,128)(2,1)}) custom-call(s32[1]{0:T(128)} %bitcast.core, f32[16,3,8,128]{3,2,1,0:T(8,128)S(1)} %all_to_all.27.mine, f32[16,3,8,128]{3,2,1,0:T(8,128)S(1)} %collective-permute-done.2.other, f32[8,4096]{1,0:T(8,128)} %bitcast.16, f32[2,8,128]{2,1,0:T(8,128)S(1)} %get-tuple-element.35.sketch_out, ...), custom_call_target="tpu_custom_call" | custom-call | bytes 5000000 | tf_op jit(solution)/shard_map/finish_out/pallas_call | solution.py:364
  72.4 3.0 %all-to-all-done.4.received = f32[16,8,128]{2,1,0:T(8,128)S(1)} async-done(((f32[16,8,128]{2,1,0:T(8,128)}), f32[16,8,128]{2,1,0:T(8,128)S(1)}, u32[]{:S(2)}, u32[]{:S(2)}) %all-to-all-start.4) | async-done | bytes 65568 | tf_op jit(solution)/shard_map/all_to_all | solution.py:360
  75.4 1.8 %finish_kv.1 = (f32[8,128]{1,0:T(8,128)}, bf16[8192,128]{1,0:T(8,128)(2,1)}) custom-call(f32[16,8,128]{2,1,0:T(8,128)S(1)} %all-to-all-done.4.received, f32[8,8,128]{2,1,0:T(8,128)S(1)} %get-tuple-element.31.lower, f32[8,128]{1,0:T(8,128)S(1)} %get-tuple-element.32.scale, f32[8,8192]{1,0:T(8,128)S(1)} %get-tuple-element.33.basis, bf16[8192,128]{1,0:T(8,128)(2,1)S(1)} %copy-done), custom_call_target="tpu_custom_call" | custom-call | bytes 5000000 | tf_op jit(solution)/shard_map/finish_kv/pallas_call | solution.py:364
  (5 shorter events, 0.1 us)
Async XLA Ops:
  3.9 17.3 %all-to-all-start = ((f32[16,2,8,128]{3,2,1,0:T(8,128)}), f32[16,2,8,128]{3,2,1,0:T(8,128)S(1)}, u32[]{:S(2)}, u32[]{:S(2)}) async-start(f32[16,2,8,128]{3,2,1,0:T(8,128)} %get-tuple-element.25), calls=%async_computation | async-start | bytes 262144 | tf_op jit(solution)/shard_map/all_to_all | solution.py:360
  18.2 4.6 %collective-permute-start = (f32[16,2,8,128]{3,2,1,0:T(8,128)S(1)}, f32[16,2,8,128]{3,2,1,0:T(8,128)S(1)}, u32[]{:S(2)}, u32[]{:S(2)}) collective-permute-start(f32[16,2,8,128]{3,2,1,0:T(8,128)S(1)} %get-tuple-element.24), channel_id=1, source_target_pairs={{0,16},{16,0},{32,48},{48,32},{64,80},{80,64},{96,112},{112,96},{1... | collective-permute-start | bytes 393224 | tf_op jit(solution)/shard_map/ppermute | solution.py:453
  21.4 2.3 %collective-permute-start.1 = (f32[16,1,8,128]{3,2,1,0:T(8,128)S(1)}, f32[16,1,8,128]{3,2,1,0:T(8,128)S(1)}, u32[]{:S(2)}, u32[]{:S(2)}) collective-permute-start(f32[16,1,8,128]{3,2,1,0:T(8,128)S(1)} %get-tuple-element.29), channel_id=1, source_target_pairs={{0,16},{16,0},{32,48},{48,32},{64,80},{80,64},{96,112},{112,96},{1... | collective-permute-start | bytes 196616 | tf_op jit(solution)/shard_map/ppermute | solution.py:454
  23.1 39.5 %copy-start = (bf16[8192,128]{1,0:T(8,128)(2,1)S(1)}, bf16[8192,128]{1,0:T(8,128)(2,1)}, u32[]{:S(2)}) copy-start(bf16[8192,128]{1,0:T(8,128)(2,1)} %get-tuple-element.30.merged_kv) | copy-start | bytes 6291460
  55.9 7.7 %collective-permute-start.2 = (f32[16,3,8,128]{3,2,1,0:T(8,128)S(1)}, f32[16,3,8,128]{3,2,1,0:T(8,128)S(1)}, u32[]{:S(2)}, u32[]{:S(2)}) collective-permute-start(f32[16,3,8,128]{3,2,1,0:T(8,128)S(1)} %all_to_all.27.mine), channel_id=1, source_target_pairs={{0,16},{16,0},{32,48},{48,32},{64,80},{80,64},{96,112},{112,96},{1... | collective-permute-start | bytes 589832 | tf_op jit(solution)/shard_map/ppermute | solution.py:460
  64.5 10.9 %all-to-all-start.4 = ((f32[16,8,128]{2,1,0:T(8,128)}), f32[16,8,128]{2,1,0:T(8,128)S(1)}, u32[]{:S(2)}, u32[]{:S(2)}) async-start(f32[16,8,128]{2,1,0:T(8,128)} %fifth_other.1), calls=%async_computation.4 | async-start | bytes 131072 | tf_op jit(solution)/shard_map/all_to_all | solution.py:360

commit v4 on v3

--- a/solution.py
+++ b/solution.py
@@ -389,12 +389,12 @@
         distant(value[0]) for value in (grad_kv, error_kv, grad_out, error_out)
     )
     kv_shape, out_shape = grad_kv.shape, grad_out.shape
-    columns = [[2 * z for z in range(8)], [2 * z + 1 for z in reversed(range(8))]]
-    replicas = [[2 * z for z in range(8)] + [2 * z + 1 for z in range(8)]]
+    columns = [[2 * z + c for z in reversed(range(8))] for c in range(2)]
+    replicas = [[15 - d for d in range(16)]]
     swap = [(d, d ^ 1) for d in range(16)]
     other_way = [15 - t for t in range(16)]
     planes = [
-        [(2 * z + c) * 16 + (t if c == 0 else other_way[t]) for t in range(16)]
+        [(2 * z + c) * 16 + other_way[t] for t in range(16)]
         for z in range(8)
         for c in range(2)
     ]

time: 77.5 us -> 73.5 us (0.948)
  waiting for transfers between devices: 7.19 us -> 4.58 us
  starting transfers between devices: 21.9 us -> 20.8 us
    all_to_all x2, waiting for transfers between devices: 5.76 us -> 2.83 us  [exchange(): return lax.all_to_all(value, axis, 0, 0, axis_index_groups=groups)]
    ppermute x1, starting transfers between devices: 6.6 us -> 4.37 us  [per_device(): other = lax.ppermute(mine, 'dp', swap)]
    all_to_all x2, starting transfers between devices: 13.7 us -> 15.8 us  [exchange(): return lax.all_to_all(value, axis, 0, 0, axis_index_groups=groups)]
    ppermute x1, starting transfers between devices: 1.35 us -> 0.08 us  [per_device(): out = keep_out + lax.ppermute(give_out, 'dp', swap)]
  transfers between devices with their start and end apart: 5 -> 5, of which waited for: 4 -> 4; matrix products, arithmetic and copies ran while one was open for 0% -> 0% of each run, Pallas kernels for 12% -> 13%
where the time goes in v4:
time: 73.5 us; the launch traced here: 73.1 us
  blocking collectives  31.7 us (43%)
  starting transfers between devices  20.8 us (28%)
  Pallas kernels  15.2 us (21%)
  waiting for transfers between devices  4.58 us (6%)
    all_to_all x3, blocking collectives, exchange(): return lax.all_to_all(value, axis, 0, 0, axis_index_groups=groups)  31.7 us
    all_to_all x2, starting transfers between devices, exchange(): return lax.all_to_all(value, axis, 0, 0, axis_index_groups=groups)  15.8 us
    pallas_call x11, Pallas kernels, call(): pl.pallas_call(kernel, out_shape=outs, in_specs=ins, out_specs=jax.tree.m...  15.2 us
    ppermute x1, starting transfers between devices, per_device(): other = lax.ppermute(mine, 'dp', swap)  4.37 us
    all_to_all x2, waiting for transfers between devices, exchange(): return lax.all_to_all(value, axis, 0, 0, axis_index_groups=groups)  2.83 us
  transfers between devices with their start and end apart: 5, of which 4 were waited for; matrix products, arithmetic and copies ran while one was open for 0% of the time, Pallas kernels for 13%

profile of v4, /device:TPU:1, one launch (start us, length us, event | category | flops | bytes accessed | tf_op | source)
XLA Modules:
  0.0 73.1 jit_solution(14090038577856272987)
XLA Ops:
  0.6 3.2 %first_out.1 = (bf16[256,4096]{1,0:T(8,128)(2,1)S(1)}, f32[16,2,8,128]{3,2,1,0:T(8,128)}) custom-call(bf16[256,4096]{1,0:T(8,128)(2,1)} %bitcast.11, bf16[256,4096]{1,0:T(8,128)(2,1)} %bitcast.12, f32[8,4096]{1,0:T(8,128)} %bitcast.15), custom_call_target="tpu_custom_call" | custom-call | bytes 5200000 | tf_op jit(solution)/shard_map/first_out/pallas_call | solution.py:364
  3.9 9.9 %all-to-all-start = ((f32[16,2,8,128]{3,2,1,0:T(8,128)}), f32[16,2,8,128]{3,2,1,0:T(8,128)S(1)}, u32[]{:S(2)}, u32[]{:S(2)}) async-start(f32[16,2,8,128]{3,2,1,0:T(8,128)} %get-tuple-element.25), calls=%async_computation | async-start | bytes 262144 | tf_op jit(solution)/shard_map/all_to_all | solution.py:360
  13.8 4.3 %first_kv.1 = (bf16[8192,128]{1,0:T(8,128)(2,1)}, bf16[256,4096]{1,0:T(8,128)(2,1)}, f32[16,2,8,128]{3,2,1,0:T(8,128)S(1)}, f32[16,2,8,128]{3,2,1,0:T(8,128)S(1)}) custom-call(s32[1]{0:T(128)} %bitcast.core, bf16[8192,128]{1,0:T(8,128)(2,1)} %bitcast.13, bf16[8192,128]{1,0:T(8,128)(2,1)} %bitcast.14, f32[8,128]{1,0:T(8,128)} %bitcast.17, ...), custom_call_target="tpu_custom_call" | custom-call | bytes 5200000 | tf_op jit(solution)/shard_map/first_kv/pallas_call | solution.py:364
  18.1 0.5 collective-permute-start
  18.6 1.6 %all-to-all-done.received = f32[16,2,8,128]{3,2,1,0:T(8,128)S(1)} async-done(((f32[16,2,8,128]{3,2,1,0:T(8,128)}), f32[16,2,8,128]{3,2,1,0:T(8,128)S(1)}, u32[]{:S(2)}, u32[]{:S(2)}) %all-to-all-start) | async-done | bytes 131104 | tf_op jit(solution)/shard_map/all_to_all | solution.py:360
  20.2 0.3 second_give.1
  20.5 0.1 collective-permute-start.1
  20.6 0.0 collective-permute-done
  20.6 0.3 second_keep.1
  20.9 0.0 copy-start
  20.9 0.9 %collective-permute-done.1 = f32[16,1,8,128]{3,2,1,0:T(8,128)S(1)} collective-permute-done((f32[16,1,8,128]{3,2,1,0:T(8,128)S(1)}, f32[16,1,8,128]{3,2,1,0:T(8,128)S(1)}, u32[]{:S(2)}, u32[]{:S(2)}) %collective-permute-start.1) | collective-permute-done | bytes 65568 | tf_op jit(solution)/shard_map/ppermute | solution.py:454
  21.8 11.5 %all_to_all.25.received = f32[16,3,8,128]{3,2,1,0:T(8,128)S(1)} all-to-all(f32[16,3,8,128]{3,2,1,0:T(8,128)S(1)} %pad_maximum_fusion), channel_id=1, replica_groups={{15,14,13,12,11,10,9,8,7,6,5,4,3,2,1,0},{31,30,29,28,27,26,25,24,23,22,..., dimensions={0} | all-to-all | bytes 393216 | tf_op jit(solution)/shard_map/all_to_all | solution.py:360
  33.4 9.9 %all_to_all.26.received = f32[8,3,8,128]{3,2,1,0:T(8,128)S(1)} all-to-all(f32[8,3,8,128]{3,2,1,0:T(8,128)S(1)} %third.1), channel_id=1, replica_groups={{224,192,160,128,96,64,32,0},{240,208,176,144,112,80,48,16},{225,193,16..., dimensions={0} | all-to-all | bytes 196608 | tf_op jit(solution)/shard_map/all_to_all | solution.py:360
  43.3 10.3 %all_to_all.27.mine = f32[16,3,8,128]{3,2,1,0:T(8,128)S(1)} all-to-all(f32[16,3,8,128]{3,2,1,0:T(8,128)S(1)} %fourth.1), channel_id=1, replica_groups={{15,14,13,12,11,10,9,8,7,6,5,4,3,2,1,0},{31,30,29,28,27,26,25,24,23,22,..., dimensions={0} | all-to-all | bytes 393216 | tf_op jit(solution)/shard_map/all_to_all | solution.py:360
  53.6 4.4 %collective-permute-start.2 = (f32[16,3,8,128]{3,2,1,0:T(8,128)S(1)}, f32[16,3,8,128]{3,2,1,0:T(8,128)S(1)}, u32[]{:S(2)}, u32[]{:S(2)}) collective-permute-start(f32[16,3,8,128]{3,2,1,0:T(8,128)S(1)} %all_to_all.27.mine), channel_id=1, source_target_pairs={{0,16},{16,0},{32,48},{48,32},{64,80},{80,64},{96,112},{112,96},{1... | collective-permute-start | bytes 589832 | tf_op jit(solution)/shard_map/ppermute | solution.py:460
  58.0 0.0 copy-done
  58.0 0.2 fifth_mine.1.begun
  58.2 0.8 %collective-permute-done.2.other = f32[16,3,8,128]{3,2,1,0:T(8,128)S(1)} collective-permute-done((f32[16,3,8,128]{3,2,1,0:T(8,128)S(1)}, f32[16,3,8,128]{3,2,1,0:T(8,128)S(1)}, u32[]{:S(2)}, u32[]{:S(2)}) %collective-permute-start.2) | collective-permute-done | bytes 196640 | tf_op jit(solution)/shard_map/ppermute | solution.py:460
  59.1 0.9 %fifth_other.1 = f32[16,8,128]{2,1,0:T(8,128)} custom-call(s32[1]{0:T(128)} %bitcast.core, f32[16,3,8,128]{3,2,1,0:T(8,128)S(1)} %collective-permute-done.2.other, bf16[8192,128]{1,0:T(8,128)(2,1)S(1)} %copy-done, f32[8,128]{1,0:T(8,128)S(1)} %fifth_mine.1.begun), custom_call_target="tpu_custom_call" | custom-call | bytes 1000000 | tf_op jit(solution)/shard_map/fifth_other/pallas_call | solution.py:364
  59.9 5.9 %all-to-all-start.4 = ((f32[16,8,128]{2,1,0:T(8,128)}), f32[16,8,128]{2,1,0:T(8,128)S(1)}, u32[]{:S(2)}, u32[]{:S(2)}) async-start(f32[16,8,128]{2,1,0:T(8,128)} %fifth_other.1), calls=%async_computation.4 | async-start | bytes 131072 | tf_op jit(solution)/shard_map/all_to_all | solution.py:360
  65.9 0.5 orthonormal_kv.1
  66.3 3.7 %finish_out.1 = (f32[8,4096]{1,0:T(8,128)}, bf16[256,4096]{1,0:T(8,128)(2,1)}) custom-call(s32[1]{0:T(128)} %bitcast.core, f32[16,3,8,128]{3,2,1,0:T(8,128)S(1)} %all_to_all.27.mine, f32[16,3,8,128]{3,2,1,0:T(8,128)S(1)} %collective-permute-done.2.other, f32[8,4096]{1,0:T(8,128)} %bitcast.16, f32[2,8,128]{2,1,0:T(8,128)S(1)} %get-tuple-element.35.sketch_out, ...), custom_call_target="tpu_custom_call" | custom-call | bytes 5000000 | tf_op jit(solution)/shard_map/finish_out/pallas_call | solution.py:364
  70.0 1.2 %all-to-all-done.4.received = f32[16,8,128]{2,1,0:T(8,128)S(1)} async-done(((f32[16,8,128]{2,1,0:T(8,128)}), f32[16,8,128]{2,1,0:T(8,128)S(1)}, u32[]{:S(2)}, u32[]{:S(2)}) %all-to-all-start.4) | async-done | bytes 65568 | tf_op jit(solution)/shard_map/all_to_all | solution.py:360
  71.3 1.8 %finish_kv.1 = (f32[8,128]{1,0:T(8,128)}, bf16[8192,128]{1,0:T(8,128)(2,1)}) custom-call(f32[16,8,128]{2,1,0:T(8,128)S(1)} %all-to-all-done.4.received, f32[8,8,128]{2,1,0:T(8,128)S(1)} %get-tuple-element.31.lower, f32[8,128]{1,0:T(8,128)S(1)} %get-tuple-element.32.scale, f32[8,8192]{1,0:T(8,128)S(1)} %get-tuple-element.33.basis, bf16[8192,128]{1,0:T(8,128)(2,1)S(1)} %copy-done), custom_call_target="tpu_custom_call" | custom-call | bytes 5000000 | tf_op jit(solution)/shard_map/finish_kv/pallas_call | solution.py:364
  (5 shorter events, 0.1 us)
Async XLA Ops:
  3.9 16.3 %all-to-all-start = ((f32[16,2,8,128]{3,2,1,0:T(8,128)}), f32[16,2,8,128]{3,2,1,0:T(8,128)S(1)}, u32[]{:S(2)}, u32[]{:S(2)}) async-start(f32[16,2,8,128]{3,2,1,0:T(8,128)} %get-tuple-element.25), calls=%async_computation | async-start | bytes 262144 | tf_op jit(solution)/shard_map/all_to_all | solution.py:360
  18.1 2.5 %collective-permute-start = (f32[16,2,8,128]{3,2,1,0:T(8,128)S(1)}, f32[16,2,8,128]{3,2,1,0:T(8,128)S(1)}, u32[]{:S(2)}, u32[]{:S(2)}) collective-permute-start(f32[16,2,8,128]{3,2,1,0:T(8,128)S(1)} %get-tuple-element.24), channel_id=1, source_target_pairs={{0,16},{16,0},{32,48},{48,32},{64,80},{80,64},{96,112},{112,96},{1... | collective-permute-start | bytes 393224 | tf_op jit(solution)/shard_map/ppermute | solution.py:453
  20.5 1.3 %collective-permute-start.1 = (f32[16,1,8,128]{3,2,1,0:T(8,128)S(1)}, f32[16,1,8,128]{3,2,1,0:T(8,128)S(1)}, u32[]{:S(2)}, u32[]{:S(2)}) collective-permute-start(f32[16,1,8,128]{3,2,1,0:T(8,128)S(1)} %get-tuple-element.29), channel_id=1, source_target_pairs={{0,16},{16,0},{32,48},{48,32},{64,80},{80,64},{96,112},{112,96},{1... | collective-permute-start | bytes 196616 | tf_op jit(solution)/shard_map/ppermute | solution.py:454
  20.9 37.1 %copy-start = (bf16[8192,128]{1,0:T(8,128)(2,1)S(1)}, bf16[8192,128]{1,0:T(8,128)(2,1)}, u32[]{:S(2)}) copy-start(bf16[8192,128]{1,0:T(8,128)(2,1)} %get-tuple-element.30.merged_kv) | copy-start | bytes 6291460
  53.6 5.4 %collective-permute-start.2 = (f32[16,3,8,128]{3,2,1,0:T(8,128)S(1)}, f32[16,3,8,128]{3,2,1,0:T(8,128)S(1)}, u32[]{:S(2)}, u32[]{:S(2)}) collective-permute-start(f32[16,3,8,128]{3,2,1,0:T(8,128)S(1)} %all_to_all.27.mine), channel_id=1, source_target_pairs={{0,16},{16,0},{32,48},{48,32},{64,80},{80,64},{96,112},{112,96},{1... | collective-permute-start | bytes 589832 | tf_op jit(solution)/shard_map/ppermute | solution.py:460
  59.9 11.3 %all-to-all-start.4 = ((f32[16,8,128]{2,1,0:T(8,128)}), f32[16,8,128]{2,1,0:T(8,128)S(1)}, u32[]{:S(2)}, u32[]{:S(2)}) async-start(f32[16,8,128]{2,1,0:T(8,128)} %fifth_other.1), calls=%async_computation.4 | async-start | bytes 131072 | tf_op jit(solution)/shard_map/all_to_all | solution.py:360

commit v5 on v4

--- a/solution.py
+++ b/solution.py
@@ -389,10 +389,10 @@
         distant(value[0]) for value in (grad_kv, error_kv, grad_out, error_out)
     )
     kv_shape, out_shape = grad_kv.shape, grad_out.shape
-    columns = [[2 * z + c for z in reversed(range(8))] for c in range(2)]
-    replicas = [[15 - d for d in range(16)]]
+    columns = [[2 * z + c for z in [6, 7, 5, 4, 3, 2, 1, 0]] for c in range(2)]
+    replicas = [[13, 15, 14, 12, 11, 10, 9, 8, 7, 6, 5, 4, 3, 2, 1, 0]]
     swap = [(d, d ^ 1) for d in range(16)]
-    other_way = [15 - t for t in range(16)]
+    other_way = [10, 15, 14, 13, 12, 11, 9, 8, 7, 6, 5, 4, 3, 2, 1, 0]
     planes = [
         [(2 * z + c) * 16 + other_way[t] for t in range(16)]
         for z in range(8)

time: 73.5 us -> 71.2 us (0.969)
  waiting for transfers between devices: 4.58 us -> 2.81 us
  blocking collectives: 31.7 us -> 30.9 us
    all_to_all x2, waiting for transfers between devices: 2.83 us -> 1.06 us  [exchange(): return lax.all_to_all(value, axis, 0, 0, axis_index_groups=groups)]
    all_to_all x2, starting transfers between devices: 15.8 us -> 16.8 us  [exchange(): return lax.all_to_all(value, axis, 0, 0, axis_index_groups=groups)]
    all_to_all x3, blocking collectives: 31.7 us -> 30.9 us  [exchange(): return lax.all_to_all(value, axis, 0, 0, axis_index_groups=groups)]
where the time goes in v5:
time: 71.2 us; the launch traced here: 70.8 us
  blocking collectives  30.9 us (43%)
  starting transfers between devices  21.2 us (30%)
  Pallas kernels  15.2 us (21%)
  waiting for transfers between devices  2.81 us (4%)
    all_to_all x3, blocking collectives, exchange(): return lax.all_to_all(value, axis, 0, 0, axis_index_groups=groups)  30.9 us
    all_to_all x2, starting transfers between devices, exchange(): return lax.all_to_all(value, axis, 0, 0, axis_index_groups=groups)  16.8 us
    pallas_call x11, Pallas kernels, call(): pl.pallas_call(kernel, out_shape=outs, in_specs=ins, out_specs=jax.tree.m...  15.2 us
    ppermute x1, starting transfers between devices, per_device(): other = lax.ppermute(mine, 'dp', swap)  3.84 us
  transfers between devices with their start and end apart: 5, of which 4 were waited for; matrix products, arithmetic and copies ran while one was open for 0% of the time, Pallas kernels for 13%

profile of v5, /device:TPU:1, one launch (start us, length us, event | category | flops | bytes accessed | tf_op | source)
XLA Modules:
  0.0 70.8 jit_solution(1595809320413168937)
XLA Ops:
  0.6 3.2 %first_out.1 = (bf16[256,4096]{1,0:T(8,128)(2,1)S(1)}, f32[16,2,8,128]{3,2,1,0:T(8,128)}) custom-call(bf16[256,4096]{1,0:T(8,128)(2,1)} %bitcast.11, bf16[256,4096]{1,0:T(8,128)(2,1)} %bitcast.12, f32[8,4096]{1,0:T(8,128)} %bitcast.15), custom_call_target="tpu_custom_call" | custom-call | bytes 5200000 | tf_op jit(solution)/shard_map/first_out/pallas_call | solution.py:364
  3.9 10.3 %all-to-all-start = ((f32[16,2,8,128]{3,2,1,0:T(8,128)}), f32[16,2,8,128]{3,2,1,0:T(8,128)S(1)}, u32[]{:S(2)}, u32[]{:S(2)}) async-start(f32[16,2,8,128]{3,2,1,0:T(8,128)} %get-tuple-element.25), calls=%async_computation | async-start | bytes 262144 | tf_op jit(solution)/shard_map/all_to_all | solution.py:360
  14.1 4.3 %first_kv.1 = (bf16[8192,128]{1,0:T(8,128)(2,1)}, bf16[256,4096]{1,0:T(8,128)(2,1)}, f32[16,2,8,128]{3,2,1,0:T(8,128)S(1)}, f32[16,2,8,128]{3,2,1,0:T(8,128)S(1)}) custom-call(s32[1]{0:T(128)} %bitcast.core, bf16[8192,128]{1,0:T(8,128)(2,1)} %bitcast.13, bf16[8192,128]{1,0:T(8,128)(2,1)} %bitcast.14, f32[8,128]{1,0:T(8,128)} %bitcast.17, ...), custom_call_target="tpu_custom_call" | custom-call | bytes 5200000 | tf_op jit(solution)/shard_map/first_kv/pallas_call | solution.py:364
  18.5 0.5 collective-permute-start
  19.0 0.7 all-to-all-done.received
  19.7 0.3 second_give.1
  20.0 0.1 collective-permute-start.1
  20.0 0.0 collective-permute-done
  20.1 0.3 second_keep.1
  20.4 0.0 copy-start
  20.4 0.9 %collective-permute-done.1 = f32[16,1,8,128]{3,2,1,0:T(8,128)S(1)} collective-permute-done((f32[16,1,8,128]{3,2,1,0:T(8,128)S(1)}, f32[16,1,8,128]{3,2,1,0:T(8,128)S(1)}, u32[]{:S(2)}, u32[]{:S(2)}) %collective-permute-start.1) | collective-permute-done | bytes 65568 | tf_op jit(solution)/shard_map/ppermute | solution.py:454
  21.3 11.2 %all_to_all.25.received = f32[16,3,8,128]{3,2,1,0:T(8,128)S(1)} all-to-all(f32[16,3,8,128]{3,2,1,0:T(8,128)S(1)} %pad_maximum_fusion), channel_id=1, replica_groups={{10,15,14,13,12,11,9,8,7,6,5,4,3,2,1,0},{26,31,30,29,28,27,25,24,23,22,..., dimensions={0} | all-to-all | bytes 393216 | tf_op jit(solution)/shard_map/all_to_all | solution.py:360
  32.5 9.8 %all_to_all.26.received = f32[8,3,8,128]{3,2,1,0:T(8,128)S(1)} all-to-all(f32[8,3,8,128]{3,2,1,0:T(8,128)S(1)} %third.1), channel_id=1, replica_groups={{192,224,160,128,96,64,32,0},{208,240,176,144,112,80,48,16},{193,225,16..., dimensions={0} | all-to-all | bytes 196608 | tf_op jit(solution)/shard_map/all_to_all | solution.py:360
  42.4 9.9 %all_to_all.27.mine = f32[16,3,8,128]{3,2,1,0:T(8,128)S(1)} all-to-all(f32[16,3,8,128]{3,2,1,0:T(8,128)S(1)} %fourth.1), channel_id=1, replica_groups={{10,15,14,13,12,11,9,8,7,6,5,4,3,2,1,0},{26,31,30,29,28,27,25,24,23,22,..., dimensions={0} | all-to-all | bytes 393216 | tf_op jit(solution)/shard_map/all_to_all | solution.py:360
  52.2 3.8 %collective-permute-start.2 = (f32[16,3,8,128]{3,2,1,0:T(8,128)S(1)}, f32[16,3,8,128]{3,2,1,0:T(8,128)S(1)}, u32[]{:S(2)}, u32[]{:S(2)}) collective-permute-start(f32[16,3,8,128]{3,2,1,0:T(8,128)S(1)} %all_to_all.27.mine), channel_id=1, source_target_pairs={{0,16},{16,0},{32,48},{48,32},{64,80},{80,64},{96,112},{112,96},{1... | collective-permute-start | bytes 589832 | tf_op jit(solution)/shard_map/ppermute | solution.py:460
  56.1 0.0 copy-done
  56.1 0.2 fifth_mine.1.begun
  56.3 0.8 %collective-permute-done.2.other = f32[16,3,8,128]{3,2,1,0:T(8,128)S(1)} collective-permute-done((f32[16,3,8,128]{3,2,1,0:T(8,128)S(1)}, f32[16,3,8,128]{3,2,1,0:T(8,128)S(1)}, u32[]{:S(2)}, u32[]{:S(2)}) %collective-permute-start.2) | collective-permute-done | bytes 196640 | tf_op jit(solution)/shard_map/ppermute | solution.py:460
  57.2 0.9 %fifth_other.1 = f32[16,8,128]{2,1,0:T(8,128)} custom-call(s32[1]{0:T(128)} %bitcast.core, f32[16,3,8,128]{3,2,1,0:T(8,128)S(1)} %collective-permute-done.2.other, bf16[8192,128]{1,0:T(8,128)(2,1)S(1)} %copy-done, f32[8,128]{1,0:T(8,128)S(1)} %fifth_mine.1.begun), custom_call_target="tpu_custom_call" | custom-call | bytes 1000000 | tf_op jit(solution)/shard_map/fifth_other/pallas_call | solution.py:364
  58.0 6.5 %all-to-all-start.4 = ((f32[16,8,128]{2,1,0:T(8,128)}), f32[16,8,128]{2,1,0:T(8,128)S(1)}, u32[]{:S(2)}, u32[]{:S(2)}) async-start(f32[16,8,128]{2,1,0:T(8,128)} %fifth_other.1), calls=%async_computation.4 | async-start | bytes 131072 | tf_op jit(solution)/shard_map/all_to_all | solution.py:360
  64.6 0.5 orthonormal_kv.1
  65.0 3.7 %finish_out.1 = (f32[8,4096]{1,0:T(8,128)}, bf16[256,4096]{1,0:T(8,128)(2,1)}) custom-call(s32[1]{0:T(128)} %bitcast.core, f32[16,3,8,128]{3,2,1,0:T(8,128)S(1)} %all_to_all.27.mine, f32[16,3,8,128]{3,2,1,0:T(8,128)S(1)} %collective-permute-done.2.other, f32[8,4096]{1,0:T(8,128)} %bitcast.16, f32[2,8,128]{2,1,0:T(8,128)S(1)} %get-tuple-element.35.sketch_out, ...), custom_call_target="tpu_custom_call" | custom-call | bytes 5000000 | tf_op jit(solution)/shard_map/finish_out/pallas_call | solution.py:364
  68.7 0.3 all-to-all-done.4.received
  69.1 1.8 %finish_kv.1 = (f32[8,128]{1,0:T(8,128)}, bf16[8192,128]{1,0:T(8,128)(2,1)}) custom-call(f32[16,8,128]{2,1,0:T(8,128)S(1)} %all-to-all-done.4.received, f32[8,8,128]{2,1,0:T(8,128)S(1)} %get-tuple-element.31.lower, f32[8,128]{1,0:T(8,128)S(1)} %get-tuple-element.32.scale, f32[8,8192]{1,0:T(8,128)S(1)} %get-tuple-element.33.basis, bf16[8192,128]{1,0:T(8,128)(2,1)S(1)} %copy-done), custom_call_target="tpu_custom_call" | custom-call | bytes 5000000 | tf_op jit(solution)/shard_map/finish_kv/pallas_call | solution.py:364
  (5 shorter events, 0.1 us)
Async XLA Ops:
  3.9 15.8 %all-to-all-start = ((f32[16,2,8,128]{3,2,1,0:T(8,128)}), f32[16,2,8,128]{3,2,1,0:T(8,128)S(1)}, u32[]{:S(2)}, u32[]{:S(2)}) async-start(f32[16,2,8,128]{3,2,1,0:T(8,128)} %get-tuple-element.25), calls=%async_computation | async-start | bytes 262144 | tf_op jit(solution)/shard_map/all_to_all | solution.py:360
  18.5 1.6 %collective-permute-start = (f32[16,2,8,128]{3,2,1,0:T(8,128)S(1)}, f32[16,2,8,128]{3,2,1,0:T(8,128)S(1)}, u32[]{:S(2)}, u32[]{:S(2)}) collective-permute-start(f32[16,2,8,128]{3,2,1,0:T(8,128)S(1)} %get-tuple-element.24), channel_id=1, source_target_pairs={{0,16},{16,0},{32,48},{48,32},{64,80},{80,64},{96,112},{112,96},{1... | collective-permute-start | bytes 393224 | tf_op jit(solution)/shard_map/ppermute | solution.py:453
  20.0 1.3 %collective-permute-start.1 = (f32[16,1,8,128]{3,2,1,0:T(8,128)S(1)}, f32[16,1,8,128]{3,2,1,0:T(8,128)S(1)}, u32[]{:S(2)}, u32[]{:S(2)}) collective-permute-start(f32[16,1,8,128]{3,2,1,0:T(8,128)S(1)} %get-tuple-element.29), channel_id=1, source_target_pairs={{0,16},{16,0},{32,48},{48,32},{64,80},{80,64},{96,112},{112,96},{1... | collective-permute-start | bytes 196616 | tf_op jit(solution)/shard_map/ppermute | solution.py:454
  20.4 35.7 %copy-start = (bf16[8192,128]{1,0:T(8,128)(2,1)S(1)}, bf16[8192,128]{1,0:T(8,128)(2,1)}, u32[]{:S(2)}) copy-start(bf16[8192,128]{1,0:T(8,128)(2,1)} %get-tuple-element.30.merged_kv) | copy-start | bytes 6291460
  52.2 4.9 %collective-permute-start.2 = (f32[16,3,8,128]{3,2,1,0:T(8,128)S(1)}, f32[16,3,8,128]{3,2,1,0:T(8,128)S(1)}, u32[]{:S(2)}, u32[]{:S(2)}) collective-permute-start(f32[16,3,8,128]{3,2,1,0:T(8,128)S(1)} %all_to_all.27.mine), channel_id=1, source_target_pairs={{0,16},{16,0},{32,48},{48,32},{64,80},{80,64},{96,112},{112,96},{1... | collective-permute-start | bytes 589832 | tf_op jit(solution)/shard_map/ppermute | solution.py:460
  58.0 11.0 %all-to-all-start.4 = ((f32[16,8,128]{2,1,0:T(8,128)}), f32[16,8,128]{2,1,0:T(8,128)S(1)}, u32[]{:S(2)}, u32[]{:S(2)}) async-start(f32[16,8,128]{2,1,0:T(8,128)} %fifth_other.1), calls=%async_computation.4 | async-start | bytes 131072 | tf_op jit(solution)/shard_map/all_to_all | solution.py:360

commit v6 on v5

--- a/solution.py
+++ b/solution.py
@@ -273,8 +273,9 @@
         basis[:, k * LANES : (k + 1) * LANES] = substitute(tile, steps, inverse)
 
 
-def finish_out(core, mine, other, warm, sketch_out, merged_out, factor, residual, near, done,
-               factor_near, warm_near, arrived, sent, factor_sent, warm_arrived):
+def finish_out(core, mine, other, warm, sketch_out, merged_out, factor, residual, basis_kv, lower_kv,
+               scale_kv, near, done, factor_near, warm_near, arrived, sent, factor_sent,
+               warm_arrived):
     wide = done.shape[1] // 4
 
     def arriving(c):
@@ -318,6 +319,8 @@
         arriving(c).wait()
         done[:, part] = (near[:, part].astype(f32) - approx).astype(bf16)
         leaving(c).start()
+
+    orthonormal_kv(core, mine, other, basis_kv, lower_kv, scale_kv)
 
     @pl.loop(0, 4)
     def _(c):
@@ -473,15 +476,15 @@
         seconds=0.5,
     )
     received = exchange(send, "dp", replicas)
-    basis, lower, scale = call(
-        orthonormal_kv,
-        (pltpu.VMEM((8, kv_shape[0]), f32), tiles(8), tiles()),
-        [scalar] + [whole] * 2,
-        (core, resident(mine), resident(other)),
-    )
-    factor_out, residual_out = call(
+    factor_out, residual_out, basis, lower, scale = call(
         finish_out,
-        (pltpu.HBM((8, out_shape[1]), f32), pltpu.HBM(out_shape, bf16)),
+        (
+            pltpu.HBM((8, out_shape[1]), f32),
+            pltpu.HBM(out_shape, bf16),
+            pltpu.VMEM((8, kv_shape[0]), f32),
+            tiles(8),
+            tiles(),
+        ),
         [scalar] + [whole] * 2 + [far, whole, far],
         (
             core,

time: 71.2 us -> 71.3 us (level)
    pallas_call x11 -> x10, Pallas kernels: 15.2 us -> 15 us  [call(): pl.pallas_call(kernel, out_shape=outs, in_specs=ins, out_specs=jax.tree.m...]
where the time goes in v6:
time: 71.3 us; the launch traced here: 70.9 us
  blocking collectives  30.9 us (43%)
  starting transfers between devices  21.2 us (30%)
  Pallas kernels  15 us (21%)
  waiting for transfers between devices  3.05 us (4%)
    all_to_all x3, blocking collectives, exchange(): return lax.all_to_all(value, axis, 0, 0, axis_index_groups=groups)  30.9 us
    all_to_all x2, starting transfers between devices, exchange(): return lax.all_to_all(value, axis, 0, 0, axis_index_groups=groups)  16.8 us
    pallas_call x10, Pallas kernels, call(): pl.pallas_call(kernel, out_shape=outs, in_specs=ins, out_specs=jax.tree.m...  15 us
    ppermute x1, starting transfers between devices, per_device(): other = lax.ppermute(mine, 'dp', swap)  3.84 us
  transfers between devices with their start and end apart: 5, of which 4 were waited for; matrix products, arithmetic and copies ran while one was open for 0% of the time, Pallas kernels for 13%

profile of v6, /device:TPU:1, one launch (start us, length us, event | category | flops | bytes accessed | tf_op | source)
XLA Modules:
  0.0 70.9 jit_solution(10269497918906081123)
XLA Ops:
  0.6 3.2 %first_out.1 = (bf16[256,4096]{1,0:T(8,128)(2,1)S(1)}, f32[16,2,8,128]{3,2,1,0:T(8,128)}) custom-call(bf16[256,4096]{1,0:T(8,128)(2,1)} %bitcast.11, bf16[256,4096]{1,0:T(8,128)(2,1)} %bitcast.12, f32[8,4096]{1,0:T(8,128)} %bitcast.15), custom_call_target="tpu_custom_call" | custom-call | bytes 5200000 | tf_op jit(solution)/shard_map/first_out/pallas_call | solution.py:367
  3.9 10.3 %all-to-all-start = ((f32[16,2,8,128]{3,2,1,0:T(8,128)}), f32[16,2,8,128]{3,2,1,0:T(8,128)S(1)}, u32[]{:S(2)}, u32[]{:S(2)}) async-start(f32[16,2,8,128]{3,2,1,0:T(8,128)} %get-tuple-element.25), calls=%async_computation | async-start | bytes 262144 | tf_op jit(solution)/shard_map/all_to_all | solution.py:363
  14.1 4.3 %first_kv.1 = (bf16[8192,128]{1,0:T(8,128)(2,1)}, bf16[256,4096]{1,0:T(8,128)(2,1)}, f32[16,2,8,128]{3,2,1,0:T(8,128)S(1)}, f32[16,2,8,128]{3,2,1,0:T(8,128)S(1)}) custom-call(s32[1]{0:T(128)} %bitcast.core, bf16[8192,128]{1,0:T(8,128)(2,1)} %bitcast.13, bf16[8192,128]{1,0:T(8,128)(2,1)} %bitcast.14, f32[8,128]{1,0:T(8,128)} %bitcast.17, ...), custom_call_target="tpu_custom_call" | custom-call | bytes 5200000 | tf_op jit(solution)/shard_map/first_kv/pallas_call | solution.py:367
  18.5 0.5 collective-permute-start
  19.0 0.7 all-to-all-done.received
  19.7 0.3 second_give.1
  20.0 0.1 collective-permute-start.1
  20.0 0.0 collective-permute-done
  20.1 0.3 second_keep.1
  20.4 0.0 copy-start
  20.4 0.9 %collective-permute-done.1 = f32[16,1,8,128]{3,2,1,0:T(8,128)S(1)} collective-permute-done((f32[16,1,8,128]{3,2,1,0:T(8,128)S(1)}, f32[16,1,8,128]{3,2,1,0:T(8,128)S(1)}, u32[]{:S(2)}, u32[]{:S(2)}) %collective-permute-start.1) | collective-permute-done | bytes 65568 | tf_op jit(solution)/shard_map/ppermute | solution.py:457
  21.3 11.2 %all_to_all.25.received = f32[16,3,8,128]{3,2,1,0:T(8,128)S(1)} all-to-all(f32[16,3,8,128]{3,2,1,0:T(8,128)S(1)} %pad_maximum_fusion), channel_id=1, replica_groups={{10,15,14,13,12,11,9,8,7,6,5,4,3,2,1,0},{26,31,30,29,28,27,25,24,23,22,..., dimensions={0} | all-to-all | bytes 393216 | tf_op jit(solution)/shard_map/all_to_all | solution.py:363
  32.5 9.8 %all_to_all.26.received = f32[8,3,8,128]{3,2,1,0:T(8,128)S(1)} all-to-all(f32[8,3,8,128]{3,2,1,0:T(8,128)S(1)} %third.1), channel_id=1, replica_groups={{192,224,160,128,96,64,32,0},{208,240,176,144,112,80,48,16},{193,225,16..., dimensions={0} | all-to-all | bytes 196608 | tf_op jit(solution)/shard_map/all_to_all | solution.py:363
  42.4 9.9 %all_to_all.27.mine = f32[16,3,8,128]{3,2,1,0:T(8,128)S(1)} all-to-all(f32[16,3,8,128]{3,2,1,0:T(8,128)S(1)} %fourth.1), channel_id=1, replica_groups={{10,15,14,13,12,11,9,8,7,6,5,4,3,2,1,0},{26,31,30,29,28,27,25,24,23,22,..., dimensions={0} | all-to-all | bytes 393216 | tf_op jit(solution)/shard_map/all_to_all | solution.py:363
  52.2 3.8 %collective-permute-start.2 = (f32[16,3,8,128]{3,2,1,0:T(8,128)S(1)}, f32[16,3,8,128]{3,2,1,0:T(8,128)S(1)}, u32[]{:S(2)}, u32[]{:S(2)}) collective-permute-start(f32[16,3,8,128]{3,2,1,0:T(8,128)S(1)} %all_to_all.27.mine), channel_id=1, source_target_pairs={{0,16},{16,0},{32,48},{48,32},{64,80},{80,64},{96,112},{112,96},{1... | collective-permute-start | bytes 589832 | tf_op jit(solution)/shard_map/ppermute | solution.py:463
  56.1 0.0 copy-done
  56.1 0.2 fifth_mine.1.begun
  56.3 0.8 %collective-permute-done.2.other = f32[16,3,8,128]{3,2,1,0:T(8,128)S(1)} collective-permute-done((f32[16,3,8,128]{3,2,1,0:T(8,128)S(1)}, f32[16,3,8,128]{3,2,1,0:T(8,128)S(1)}, u32[]{:S(2)}, u32[]{:S(2)}) %collective-permute-start.2) | collective-permute-done | bytes 196640 | tf_op jit(solution)/shard_map/ppermute | solution.py:463
  57.2 0.9 %fifth_other.1 = f32[16,8,128]{2,1,0:T(8,128)} custom-call(s32[1]{0:T(128)} %bitcast.core, f32[16,3,8,128]{3,2,1,0:T(8,128)S(1)} %collective-permute-done.2.other, bf16[8192,128]{1,0:T(8,128)(2,1)S(1)} %copy-done, f32[8,128]{1,0:T(8,128)S(1)} %fifth_mine.1.begun), custom_call_target="tpu_custom_call" | custom-call | bytes 1000000 | tf_op jit(solution)/shard_map/fifth_other/pallas_call | solution.py:367
  58.0 6.5 %all-to-all-start.4 = ((f32[16,8,128]{2,1,0:T(8,128)}), f32[16,8,128]{2,1,0:T(8,128)S(1)}, u32[]{:S(2)}, u32[]{:S(2)}) async-start(f32[16,8,128]{2,1,0:T(8,128)} %fifth_other.1), calls=%async_computation.4 | async-start | bytes 131072 | tf_op jit(solution)/shard_map/all_to_all | solution.py:363
  64.6 3.9 %finish_out.1 = (f32[8,4096]{1,0:T(8,128)}, bf16[256,4096]{1,0:T(8,128)(2,1)}, f32[8,8192]{1,0:T(8,128)S(1)}, f32[8,8,128]{2,1,0:T(8,128)S(1)}, f32[8,128]{1,0:T(8,128)S(1)}) custom-call(s32[1]{0:T(128)} %bitcast.core, f32[16,3,8,128]{3,2,1,0:T(8,128)S(1)} %all_to_all.27.mine, f32[16,3,8,128]{3,2,1,0:T(8,128)S(1)} %collective-permute-done.2.other, ...), custom_call_target="tpu_custom_call" | custom-call | bytes 5000000 | tf_op jit(solution)/shard_map/finish_out/pallas_call | solution.py:367
  68.5 0.6 all-to-all-done.4.received
  69.1 1.8 %finish_kv.1 = (f32[8,128]{1,0:T(8,128)}, bf16[8192,128]{1,0:T(8,128)(2,1)}) custom-call(f32[16,8,128]{2,1,0:T(8,128)S(1)} %all-to-all-done.4.received, f32[8,8,128]{2,1,0:T(8,128)S(1)} %get-tuple-element.33.lower, f32[8,128]{1,0:T(8,128)S(1)} %get-tuple-element.34.scale, f32[8,8192]{1,0:T(8,128)S(1)} %get-tuple-element.35.basis, bf16[8192,128]{1,0:T(8,128)(2,1)S(1)} %copy-done), custom_call_target="tpu_custom_call" | custom-call | bytes 5000000 | tf_op jit(solution)/shard_map/finish_kv/pallas_call | solution.py:367
  (5 shorter events, 0.1 us)
Async XLA Ops:
  3.9 15.8 %all-to-all-start = ((f32[16,2,8,128]{3,2,1,0:T(8,128)}), f32[16,2,8,128]{3,2,1,0:T(8,128)S(1)}, u32[]{:S(2)}, u32[]{:S(2)}) async-start(f32[16,2,8,128]{3,2,1,0:T(8,128)} %get-tuple-element.25), calls=%async_computation | async-start | bytes 262144 | tf_op jit(solution)/shard_map/all_to_all | solution.py:363
  18.5 1.6 %collective-permute-start = (f32[16,2,8,128]{3,2,1,0:T(8,128)S(1)}, f32[16,2,8,128]{3,2,1,0:T(8,128)S(1)}, u32[]{:S(2)}, u32[]{:S(2)}) collective-permute-start(f32[16,2,8,128]{3,2,1,0:T(8,128)S(1)} %get-tuple-element.24), channel_id=1, source_target_pairs={{0,16},{16,0},{32,48},{48,32},{64,80},{80,64},{96,112},{112,96},{1... | collective-permute-start | bytes 393224 | tf_op jit(solution)/shard_map/ppermute | solution.py:456
  20.0 1.3 %collective-permute-start.1 = (f32[16,1,8,128]{3,2,1,0:T(8,128)S(1)}, f32[16,1,8,128]{3,2,1,0:T(8,128)S(1)}, u32[]{:S(2)}, u32[]{:S(2)}) collective-permute-start(f32[16,1,8,128]{3,2,1,0:T(8,128)S(1)} %get-tuple-element.29), channel_id=1, source_target_pairs={{0,16},{16,0},{32,48},{48,32},{64,80},{80,64},{96,112},{112,96},{1... | collective-permute-start | bytes 196616 | tf_op jit(solution)/shard_map/ppermute | solution.py:457
  20.4 35.7 %copy-start = (bf16[8192,128]{1,0:T(8,128)(2,1)S(1)}, bf16[8192,128]{1,0:T(8,128)(2,1)}, u32[]{:S(2)}) copy-start(bf16[8192,128]{1,0:T(8,128)(2,1)} %get-tuple-element.30.merged_kv) | copy-start | bytes 6291460
  52.2 4.9 %collective-permute-start.2 = (f32[16,3,8,128]{3,2,1,0:T(8,128)S(1)}, f32[16,3,8,128]{3,2,1,0:T(8,128)S(1)}, u32[]{:S(2)}, u32[]{:S(2)}) collective-permute-start(f32[16,3,8,128]{3,2,1,0:T(8,128)S(1)} %all_to_all.27.mine), channel_id=1, source_target_pairs={{0,16},{16,0},{32,48},{48,32},{64,80},{80,64},{96,112},{112,96},{1... | collective-permute-start | bytes 589832 | tf_op jit(solution)/shard_map/ppermute | solution.py:463
  58.0 11.0 %all-to-all-start.4 = ((f32[16,8,128]{2,1,0:T(8,128)}), f32[16,8,128]{2,1,0:T(8,128)S(1)}, u32[]{:S(2)}, u32[]{:S(2)}) async-start(f32[16,8,128]{2,1,0:T(8,128)} %fifth_other.1), calls=%async_computation.4 | async-start | bytes 131072 | tf_op jit(solution)/shard_map/all_to_all | solution.py:363
